TPU v7x, 32 devices: a whole 2x2x4 slice. The times are simulated.
32 devices in a mesh: curve: 8 (over y, x, core), sub: 4 (over z).
Axes of the slice: x: 2, y: 2, z: 4, core: 2. Of those that a mesh axis runs over, the one named last changes fastest.
Arguments:
- fields: float32 [96, 5, 16, 256], P(('curve', 'sub'))
- new_source: int32 [96], replicated, may hold values from -1 to 95, as said below
- ghost_source: int32 [96, 6], replicated, may hold values from -1 to 95, as said below
Outputs:
- advanced_fields: float32 [96, 5, 16, 256], P(('curve', 'sub'))
Inputs may be any that keep to these rules, and one draw needn't show every extreme that they name: `new_source`: entry j names the slot whose box slot j holds after the regrid, or -1 where slot j is empty. Slots are numbered segment by segment along the curve (3 a segment). The named slot lies on the same curve segment or on one next to it (the curve does not close), no slot is named twice, every segment holds at least one box, and at most one box goes from one segment to one neighbouring segment, exactly one for some pair. `ghost_source`: entries are -1 exactly for the faces of empty slots (new_source -1); every other entry names an occupied slot on a curve segment at most 2 away along the curve, which here closes on itself. The faces of one segment draw on one segment, itself included, at most 4 times, exactly 4 times for some pair.
All inputs are finite; a program needn't handle non-finite values.
Results may differ from a plain program's by a relative error of at most 0.0003.
Values sent between devices are 32-bit elements; how exact they have to be, the bound alone decides.
A program may use at most 64 MiB of HBM per device.

v0:
```python
import jax
import jax.numpy as jnp
from jax import lax
from jax.sharding import PartitionSpec as P

GHOST = 2
REACH = 2
CAPG = 4


GAMMA = 5.0 / 3.0
COURANT = 0.3
FILLER = (1.0, 0.0, 0.0, 0.0, 1.5)


def passed_along(block, axis, distance):
    devices = range(lax.axis_size(axis))
    route = [(i - distance, i) for i in devices if i - distance in devices]
    return lax.ppermute(block, axis, route)


def passed_along_2(value, axis, steps):
    count = lax.axis_size(axis)
    pairs = [(source, (source + steps) % count) for source in range(count)]
    return lax.ppermute(value, axis, pairs)


def filler(trailing):
    return jnp.array(FILLER, jnp.float32).reshape((5,) + (1,) * trailing)


def minmod(lower_step, upper_step):
    return (
        0.5
        * (jnp.sign(lower_step) + jnp.sign(upper_step))
        * jnp.minimum(jnp.abs(lower_step), jnp.abs(upper_step))
    )


def primitives(state):
    density = state[:, 0]
    vel_x = state[:, 1] / density
    vel_y = state[:, 2] / density
    vel_z = state[:, 3] / density
    kinetic = 0.5 * density * (vel_x * vel_x + vel_y * vel_y + vel_z * vel_z)
    pressure = (GAMMA - 1.0) * (state[:, 4] - kinetic)
    return [density, vel_x, vel_y, vel_z, pressure]


def euler_terms(primitive, normal):
    density, vel_x, vel_y, vel_z, pressure = primitive
    along = primitive[normal]
    energy = pressure / (GAMMA - 1.0) + 0.5 * density * (
        vel_x * vel_x + vel_y * vel_y + vel_z * vel_z
    )
    conserved = [density, density * vel_x, density * vel_y, density * vel_z, energy]
    fluxes = [value * along for value in conserved]
    fluxes[normal] = fluxes[normal] + pressure
    fluxes[4] = fluxes[4] + pressure * along
    speeds = jnp.abs(along) + jnp.sqrt(GAMMA * pressure / density)
    return (conserved, fluxes, speeds)


def flux_sweep(primitive, axis_index, normal):
    interior = primitive[0].shape[axis_index] - 4

    def cut_range(array_in, start_at, stop_at):
        return lax.slice_in_dim(array_in, start_at, stop_at, axis=axis_index)

    lefts = []
    rights = []
    for values in primitive:
        steps = cut_range(values, 1, interior + 4) - cut_range(values, 0, interior + 3)
        slope = minmod(cut_range(steps, 0, interior + 2), cut_range(steps, 1, interior + 3))
        lefts.append(cut_range(values, 1, interior + 2) + 0.5 * cut_range(slope, 0, interior + 1))
        rights.append(cut_range(values, 2, interior + 3) - 0.5 * cut_range(slope, 1, interior + 2))
    cons_left, flux_left, speed_left = euler_terms(lefts, normal)
    cons_right, flux_right, speed_right = euler_terms(rights, normal)
    wave_speed = jnp.maximum(speed_left, speed_right)
    differences = []
    for field_index in range(5):
        face_flux = 0.5 * (flux_left[field_index] + flux_right[field_index]) - 0.5 * wave_speed * (
            cons_right[field_index] - cons_left[field_index]
        )
        differences.append(
            cut_range(face_flux, 1, interior + 1) - cut_range(face_flux, 0, interior)
        )
    return jnp.stack(differences, axis=1)


def side_strips(box_cells):
    box_edge = box_cells.shape[-1]
    low_x = jnp.swapaxes(box_cells[..., :GHOST], -1, -2)
    high_x = jnp.swapaxes(box_cells[..., box_edge - GHOST :], -1, -2)
    low_y = box_cells[..., :GHOST, :]
    high_y = box_cells[..., box_edge - GHOST :, :]
    low_z = jnp.swapaxes(box_cells[:, :, :GHOST], 2, 3)
    high_z = jnp.swapaxes(box_cells[:, :, box_edge - GHOST :], 2, 3)
    return jnp.stack([low_x, high_x, low_y, high_y, low_z, high_z], axis=1)


def fastest(box_cells, occupied):
    primitive = primitives(box_cells)
    sound = jnp.sqrt(GAMMA * primitive[4] / primitive[0])
    quickest = (
        jnp.maximum(
            jnp.maximum(jnp.abs(primitive[1]), jnp.abs(primitive[2])), jnp.abs(primitive[3])
        )
        + sound
    )
    return jnp.max(jnp.where(occupied[:, None, None, None], quickest, 0.0))


def advance(box_cells, ghosts, time_ratio, occupied):
    along_x = jnp.concatenate(
        [jnp.swapaxes(ghosts[:, 0], -1, -2), box_cells, jnp.swapaxes(ghosts[:, 1], -1, -2)], axis=4
    )
    along_y = jnp.concatenate([ghosts[:, 2], box_cells, ghosts[:, 3]], axis=3)
    along_z = jnp.concatenate(
        [jnp.swapaxes(ghosts[:, 4], 2, 3), box_cells, jnp.swapaxes(ghosts[:, 5], 2, 3)], axis=2
    )
    summed = flux_sweep(primitives(along_x), 3, 1) + flux_sweep(primitives(along_y), 2, 2)
    summed = summed + flux_sweep(primitives(along_z), 1, 3)
    updated = box_cells - time_ratio * summed
    return jnp.where(occupied[:, None, None, None, None], updated, 0.0)


def face_sides(slot_count):
    return jnp.tile(jnp.array([1, 0, 3, 2, 5, 4], jnp.int32), slot_count)


def pack_for(strips, ghost_source, receiver, sender, slot_count):
    wanted = lax.dynamic_slice_in_dim(ghost_source, receiver * slot_count, slot_count).reshape(-1)
    going = (wanted >= 0) & (wanted // slot_count == sender)
    send_rank = jnp.cumsum(going.astype(jnp.int32)) - 1
    choose = going[None, :] & (send_rank[None, :] == jnp.arange(CAPG, dtype=jnp.int32)[:, None])
    strip_index = wanted % slot_count * 6 + face_sides(slot_count)
    row_index = jnp.sum(jnp.where(choose, strip_index[None, :], 0), axis=1)
    return jnp.take(strips, row_index, axis=0)


def unpack(ghosts, incoming, wanted, offset, shift_by):
    matches = (wanted >= 0) & (offset == shift_by)
    recv_rank = jnp.cumsum(matches.astype(jnp.int32)) - 1
    delivered = jnp.take(incoming, jnp.clip(recv_rank, 0, CAPG - 1), axis=0)
    return jnp.where(matches[:, None, None, None, None], delivered, ghosts)


def body(fields, new_source, ghost_source):
    slot_count, field_count, box_edge, cells = fields.shape
    curve_count = lax.axis_size(("curve", "sub"))
    position = lax.axis_index(("curve", "sub"))
    own_sources = lax.dynamic_slice_in_dim(new_source, position * slot_count, slot_count)
    occupied = own_sources >= 0
    old_owner = jnp.where(occupied, own_sources // slot_count, -5)
    from_slot = own_sources % slot_count
    sources_pool = [fields]
    for shift_by in (1, -1):
        sources_pool.append(passed_along(fields, ("curve", "sub"), shift_by))
    anchor = jnp.where(old_owner == position, 0, jnp.where(old_owner == position - 1, 1, 2))
    chosen_rows = anchor * slot_count + from_slot
    candidates = jnp.concatenate(sources_pool, axis=0)
    moved_boxes = jnp.take(candidates, chosen_rows, axis=0)
    moved_boxes = jnp.where(occupied[:, None, None, None], moved_boxes, filler(2))
    box_cells = moved_boxes.reshape(slot_count, field_count, box_edge, box_edge, box_edge)
    fastest_speed = lax.pmax(fastest(box_cells, occupied), ("curve", "sub"))
    time_ratio = COURANT / fastest_speed
    strips = side_strips(box_cells).reshape(slot_count * 6, field_count, box_edge, GHOST, box_edge)
    wanted = lax.dynamic_slice_in_dim(ghost_source, position * slot_count, slot_count).reshape(-1)
    is_valid = wanted >= 0
    source_owner = wanted // slot_count
    offset = (position - source_owner + REACH) % curve_count - REACH
    ghosts = jnp.broadcast_to(filler(3), (slot_count * 6, field_count, box_edge, GHOST, box_edge))
    local_face = is_valid & (offset == 0)
    local_rows = wanted % slot_count * 6 + face_sides(slot_count)
    ghosts = jnp.where(
        local_face[:, None, None, None, None], jnp.take(strips, local_rows, axis=0), ghosts
    )
    distances = [shift_by for shift_by in range(-REACH, REACH + 1) if shift_by != 0]
    for shift_by in distances:
        receiver = (position + shift_by) % curve_count
        packed_faces = pack_for(strips, ghost_source, receiver, position, slot_count)
        incoming = passed_along_2(packed_faces, ("curve", "sub"), shift_by)
        ghosts = unpack(ghosts, incoming, wanted, offset, shift_by)
    ghosts = ghosts.reshape(slot_count, 6, field_count, box_edge, GHOST, box_edge)

    def advance_slot(slot_item):
        cells_one, ghosts_one, occupied_one = slot_item
        return advance(cells_one[None], ghosts_one[None], time_ratio, occupied_one[None])[0]

    result = lax.map(advance_slot, (box_cells, ghosts, occupied))
    return result.reshape(slot_count, field_count, box_edge, cells)


def solution(mesh):
    placed = (P(("curve", "sub"), None, None, None), P(), P())
    return jax.shard_map(
        body,
        mesh=mesh,
        in_specs=placed,
        out_specs=P(("curve", "sub"), None, None, None),
        check_vma=False,
    )
```

profile of v0, /device:TPU:0, one launch (start us, length us, event | category | flops | bytes accessed | tf_op | source)
XLA Modules:
  0.0 175.9 jit_solution(15187952259970881792)
XLA Ops:
  0.0 4.9 %collective-permute-start = (f32[3,5,16,256]{3,2,1,0:T(8,128)}, f32[3,5,16,256]{3,2,1,0:T(8,128)S(1)}, u32[]{:S(2)}, u32[]{:S(2)}) collective-permute-start(f32[3,5,16,256]{3,2,1,0:T(8,128)} %param.16), channel_id=1, source_target_pairs={{0,1},{1,2},{2,3},{3,4},{4,5},{5,6},{6,7},{7,8},{8,9},{9,10},{10,1... | collective-permute-start | bytes 737288 | tf_op jit(solution)/shard_map/ppermute | solution.py:19
  4.9 1.3 collective-permute-start.1
  6.3 1.0 dynamic-slice_compare_fusion.3
  7.3 1.0 dynamic-slice_divide_fusion.3
  17.6 1.6 collective-permute-done.1
  19.2 1.0 pad_maximum_fusion.3
  20.8 1.9 %gather.17 = f32[3,5,16,16,16]{4,3,2,1,0:T(8,128)} reshape(f32[3,5,16,256]{3,2,1,0:T(8,128)S(1)} %gather_fusion) | data formatting | bytes 491520 | tf_op jit(solution)/shard_map/jit(_take)/gather | solution.py:163
  22.7 1.9 %select_select_fusion = f32[3,5,16,16,16]{4,3,2,1,0:T(8,128)S(1)} fusion(f32[3,5,16,16,16]{4,3,2,1,0:T(8,128)} %gather.17, f32[5]{0:T(128)S(1)} %copy-done.7, pred[3]{0:T(512)(128)(4,1)S(1)} %get-tuple-element.98, pred[3]{0:T(512)(128)(4,1)S(1)} %get-tuple-element.342), kind=kLoop, calls=%fused_computation.210 | loop fusion | flops 122880 | bytes 491546 | tf_op jit(solution)/shard_map/jit(_where)/select_n | solution.py:164
  24.6 2.6 %fusion.159 = (f32[3,5,16,16,2]{4,3,2,1,0:T(8,128)}, f32[3,5,16,16,2]{4,3,2,1,0:T(8,128)}) fusion(f32[3,5,16,16,16]{4,3,2,1,0:T(8,128)S(1)} %select_select_fusion), kind=kLoop, calls=%fused_computation.395 | loop fusion | bytes 122880 | tf_op jit(solution)/shard_map/slice | solution.py:94
  27.4 3.0 %copy.245 = f32[3,5,16,16,2]{3,2,4,1,0:T(8,128)S(1)} copy(f32[3,5,16,16,2]{4,3,2,1,0:T(8,128)} %get-tuple-element.133) | data formatting | bytes 61440
  31.2 3.0 %copy.246 = f32[3,5,16,16,2]{3,2,4,1,0:T(8,128)S(1)} copy(f32[3,5,16,16,2]{4,3,2,1,0:T(8,128)} %get-tuple-element.132) | data formatting | bytes 61440
  37.8 1.5 copy.200
  39.3 1.3 gather_fusion.2
  40.6 1.8 %broadcast_select_fusion.3 = f32[4,5,16,2,16]{4,2,3,1,0:T(8,128)} fusion(f32[4,5,16,2,16]{4,2,3,1,0:T(8,128)} %gather_fusion.2, pred[4]{0:T(512)(128)(4,1)S(1)} %compare_and_fusion.11), kind=kLoop, calls=%fused_computation.244 | loop fusion | flops 10240 | bytes 81924 | tf_op jit(solution)/shard_map/jit(_take)/select_n | solution.py:139
  42.4 2.0 %collective-permute-start.2 = (f32[4,5,16,2,16]{4,2,3,1,0:T(8,128)}, f32[4,5,16,2,16]{4,2,3,1,0:T(8,128)}, u32[]{:S(2)}, u32[]{:S(2)}) collective-permute-start(f32[4,5,16,2,16]{4,2,3,1,0:T(8,128)} %broadcast_select_fusion.3), channel_id=1, source_target_pairs={{0,2},{1,3},{2,4},{3,5},{4,6},{5,7},{6,8},{7,9},{8,10},{9,11},{10,... | collective-permute-start | bytes 122888 | tf_op jit(solution)/shard_map/ppermute | solution.py:25
  44.4 1.3 gather_fusion.4
  45.7 1.8 %broadcast_select_fusion.2 = f32[4,5,16,2,16]{4,2,3,1,0:T(8,128)} fusion(f32[4,5,16,2,16]{4,2,3,1,0:T(8,128)} %gather_fusion.4, pred[4]{0:T(512)(128)(4,1)S(1)} %compare_and_fusion.9), kind=kLoop, calls=%fused_computation.243 | loop fusion | flops 10240 | bytes 81924 | tf_op jit(solution)/shard_map/jit(_take)/select_n | solution.py:139
  47.5 1.6 collective-permute-start.3
  49.1 1.3 gather_fusion.6
  50.4 1.8 %broadcast_select_fusion.1 = f32[4,5,16,2,16]{4,2,3,1,0:T(8,128)} fusion(f32[4,5,16,2,16]{4,2,3,1,0:T(8,128)} %gather_fusion.6, pred[4]{0:T(512)(128)(4,1)S(1)} %compare_and_fusion.7), kind=kLoop, calls=%fused_computation.242 | loop fusion | flops 10240 | bytes 81924 | tf_op jit(solution)/shard_map/jit(_take)/select_n | solution.py:139
  52.3 3.8 %collective-permute-start.4 = (f32[4,5,16,2,16]{4,2,3,1,0:T(8,128)}, f32[4,5,16,2,16]{4,2,3,1,0:T(8,128)}, u32[]{:S(2)}, u32[]{:S(2)}) collective-permute-start(f32[4,5,16,2,16]{4,2,3,1,0:T(8,128)} %broadcast_select_fusion.1), channel_id=1, source_target_pairs={{0,31},{1,0},{2,1},{3,2},{4,3},{5,4},{6,5},{7,6},{8,7},{9,8},{10,9... | collective-permute-start | bytes 122888 | tf_op jit(solution)/shard_map/ppermute | solution.py:25
  56.0 1.3 gather_fusion.8
  57.4 1.8 %broadcast_select_fusion = f32[4,5,16,2,16]{4,2,3,1,0:T(8,128)} fusion(f32[4,5,16,2,16]{4,2,3,1,0:T(8,128)} %gather_fusion.8, pred[4]{0:T(512)(128)(4,1)S(1)} %compare_and_fusion.5), kind=kLoop, calls=%fused_computation.241 | loop fusion | flops 10240 | bytes 81924 | tf_op jit(solution)/shard_map/jit(_take)/select_n | solution.py:139
  59.2 1.0 fusion.93
  60.2 49.2 %pmax.7 = f32[]{:T(128)} all-reduce(f32[]{:T(128)} %fusion.93), channel_id=1, replica_groups=mesh['curve'=8,'sub'=4] {'curve','sub'}, use_global_device_ids=true, to_apply=%region_13.16 | all-reduce | flops 1 | bytes 8 | tf_op jit(solution)/shard_map/pmax | solution.py:166
  109.4 1.8 gather_fusion.1
  111.8 2.7 %gather_fusion.3 = f32[18,5,16,2,16]{4,2,3,1,0:T(8,128)} fusion(f32[4,5,16,2,16]{4,2,3,1,0:T(8,128)} %collective-permute-done.2, s32[1024]{0:T(1024)S(1)} %get-tuple-element.182), kind=kCustom, calls=%fused_computation.1.clone | custom fusion | bytes 368712 | tf_op jit(solution)/shard_map/jit(_take)/gather | solution.py:145
  114.6 2.7 %gather_fusion.5 = f32[18,5,16,2,16]{4,2,3,1,0:T(8,128)} fusion(f32[4,5,16,2,16]{4,2,3,1,0:T(8,128)} %collective-permute-done.3, s32[1024]{0:T(1024)S(1)} %get-tuple-element.181), kind=kCustom, calls=%fused_computation.5.clone | custom fusion | bytes 368712 | tf_op jit(solution)/shard_map/jit(_take)/gather | solution.py:145
  117.3 2.7 %gather_fusion.7 = f32[18,5,16,2,16]{4,2,3,1,0:T(8,128)} fusion(f32[4,5,16,2,16]{4,2,3,1,0:T(8,128)} %collective-permute-done.4, s32[1024]{0:T(1024)S(1)} %get-tuple-element.180), kind=kCustom, calls=%fused_computation.6.clone | custom fusion | bytes 368712 | tf_op jit(solution)/shard_map/jit(_take)/gather | solution.py:145
  120.0 2.8 %gather_fusion.9 = f32[18,5,16,2,16]{4,2,3,1,0:T(8,128)} fusion(f32[4,5,16,2,16]{4,2,3,1,0:T(8,128)} %collective-permute-done.5, s32[1024]{0:T(1024)S(1)} %get-tuple-element.179), kind=kCustom, calls=%fused_computation.7.clone | custom fusion | bytes 368712 | tf_op jit(solution)/shard_map/jit(_take)/gather | solution.py:145
  122.8 4.8 %fusion.83 = f32[18,5,16,2,16]{4,2,3,1,0:T(8,128)S(1)} fusion(f32[18,5,16,2,16]{4,2,3,1,0:T(8,128)} %gather_fusion.9, f32[18,5,16,2,16]{4,2,3,1,0:T(8,128)} %gather_fusion.7, f32[18,5,16,2,16]{4,2,3,1,0:T(8,128)} %gather_fusion.5, f32[18,5,16,2,16]{4,2,3,1,0:T(8,128)} %gather_fusion.3, f32[18,5,16,2,16]{4,2,3,1,0:T(8,128)} %gather_fusion.1, ...), kind=kLoop, calls=%fused_computation.214 | loop fusion | flops 460800 | bytes 1106120 | tf_op jit(solution)/shard_map/jit(_where)/select_n | solution.py:146
  127.7 45.2 %while.10 = (s32[]{:T(128)}, f32[3,5,16,16,16]{4,3,2,1,0:T(8,128)}, pred[3]{0:T(512)(128)(4,1)S(1)}, f32[3,5,16,16,16]{4,3,2,1,0:T(8,128)S(1)}, f32[]{:T(128)}, ...) while((s32[]{:T(128)}, f32[3,5,16,16,16]{4,3,2,1,0:T(8,128)}, ...), condition=%wide.region_15.18_spmd, body=%wide.region_14.17_spmd.sunk | while | flops 2472452 | bytes 14266271 | solution.py:191
  127.7 0.8 dynamic-slice_bitcast_fusion.7
  131.4 0.8 copy-done
  132.8 1.4 copy.260
  134.2 1.5 pad_maximum_fusion.8
  140.9 1.8 %select_dynamic-update-slice_fusion.2 = f32[3,5,16,16,16]{4,3,2,1,0:T(8,128)} fusion(f32[3,5,16,16,16]{4,3,2,1,0:T(8,128)} %get-tuple-element.354, s32[]{:T(128)} %get-tuple-element.353, f32[1,5,16,16,16]{4,3,2,1,0:T(8,128)S(1)} %fusion.187, f32[1,5,16,16,16]{4,3,2,1,0:T(8,128)S(1)} %fusion.194, f32[1,5,16,16,16]{4,3,2,1,0:T(8,128)S(1)} %copy-done.1, ...), kind=kLoop, calls=%fused_computation.13.clone.1 | loop fusion | flops 102400 | bytes 984576 | tf_op jit(solution)/shard_map/while/body/jit(dynamic_update_index_in_dim)/dynamic_update_slice | solution.py:191
  142.7 0.8 dynamic-slice_bitcast_fusion.7
  146.5 0.8 copy-done
  147.8 1.4 copy.260
  149.2 1.5 pad_maximum_fusion.8
  156.0 1.8 %select_dynamic-update-slice_fusion.2 = f32[3,5,16,16,16]{4,3,2,1,0:T(8,128)} fusion(f32[3,5,16,16,16]{4,3,2,1,0:T(8,128)} %get-tuple-element.354, s32[]{:T(128)} %get-tuple-element.353, f32[1,5,16,16,16]{4,3,2,1,0:T(8,128)S(1)} %fusion.187, f32[1,5,16,16,16]{4,3,2,1,0:T(8,128)S(1)} %fusion.194, f32[1,5,16,16,16]{4,3,2,1,0:T(8,128)S(1)} %copy-done.1, ...), kind=kLoop, calls=%fused_computation.13.clone.1 | loop fusion | flops 102400 | bytes 984576 | tf_op jit(solution)/shard_map/while/body/jit(dynamic_update_index_in_dim)/dynamic_update_slice | solution.py:191
  157.8 0.8 dynamic-slice_bitcast_fusion.7
  161.5 0.8 copy-done
  162.9 1.4 copy.260
  164.3 1.5 pad_maximum_fusion.8
  171.1 1.8 %select_dynamic-update-slice_fusion.2 = f32[3,5,16,16,16]{4,3,2,1,0:T(8,128)} fusion(f32[3,5,16,16,16]{4,3,2,1,0:T(8,128)} %get-tuple-element.354, s32[]{:T(128)} %get-tuple-element.353, f32[1,5,16,16,16]{4,3,2,1,0:T(8,128)S(1)} %fusion.187, f32[1,5,16,16,16]{4,3,2,1,0:T(8,128)S(1)} %fusion.194, f32[1,5,16,16,16]{4,3,2,1,0:T(8,128)S(1)} %copy-done.1, ...), kind=kLoop, calls=%fused_computation.13.clone.1 | loop fusion | flops 102400 | bytes 984576 | tf_op jit(solution)/shard_map/while/body/jit(dynamic_update_index_in_dim)/dynamic_update_slice | solution.py:191
  172.9 3.0 %reshape.1704 = f32[3,5,16,256]{3,2,1,0:T(8,128)} reshape(f32[3,5,16,16,16]{4,3,2,1,0:T(8,128)} %get-tuple-element.39) | data formatting | bytes 491520 | tf_op jit(solution)/shard_map/reshape | solution.py:192
  (348 shorter events, 39.2 us)
Async XLA Ops:
  0.0 17.6 %collective-permute-start = (f32[3,5,16,256]{3,2,1,0:T(8,128)}, f32[3,5,16,256]{3,2,1,0:T(8,128)S(1)}, u32[]{:S(2)}, u32[]{:S(2)}) collective-permute-start(f32[3,5,16,256]{3,2,1,0:T(8,128)} %param.16), channel_id=1, source_target_pairs={{0,1},{1,2},{2,3},{3,4},{4,5},{5,6},{6,7},{7,8},{8,9},{9,10},{10,1... | collective-permute-start | bytes 737288 | tf_op jit(solution)/shard_map/ppermute | solution.py:19
  4.9 14.3 %collective-permute-start.1 = (f32[3,5,16,256]{3,2,1,0:T(8,128)}, f32[3,5,16,256]{3,2,1,0:T(8,128)S(1)}, u32[]{:S(2)}, u32[]{:S(2)}) collective-permute-start(f32[3,5,16,256]{3,2,1,0:T(8,128)} %param.16), channel_id=1, source_target_pairs={{1,0},{2,1},{3,2},{4,3},{5,4},{6,5},{7,6},{8,7},{9,8},{10,9},{11,1... | collective-permute-start | bytes 737288 | tf_op jit(solution)/shard_map/ppermute | solution.py:19
  20.2 2.5 %copy-start.7 = (f32[5]{0:T(128)S(1)}, f32[5]{0:T(128)}, u32[]{:S(2)}) copy-start(f32[5]{0:T(128)} %constant.244.clone) | copy-start | bytes 64
  42.4 69.5 %collective-permute-start.2 = (f32[4,5,16,2,16]{4,2,3,1,0:T(8,128)}, f32[4,5,16,2,16]{4,2,3,1,0:T(8,128)}, u32[]{:S(2)}, u32[]{:S(2)}) collective-permute-start(f32[4,5,16,2,16]{4,2,3,1,0:T(8,128)} %broadcast_select_fusion.3), channel_id=1, source_target_pairs={{0,2},{1,3},{2,4},{3,5},{4,6},{5,7},{6,8},{7,9},{8,10},{9,11},{10,... | collective-permute-start | bytes 122888 | tf_op jit(solution)/shard_map/ppermute | solution.py:25
  47.5 67.0 %collective-permute-start.3 = (f32[4,5,16,2,16]{4,2,3,1,0:T(8,128)}, f32[4,5,16,2,16]{4,2,3,1,0:T(8,128)}, u32[]{:S(2)}, u32[]{:S(2)}) collective-permute-start(f32[4,5,16,2,16]{4,2,3,1,0:T(8,128)} %broadcast_select_fusion.2), channel_id=1, source_target_pairs={{0,1},{1,2},{2,3},{3,4},{4,5},{5,6},{6,7},{7,8},{8,9},{9,10},{10,1... | collective-permute-start | bytes 122888 | tf_op jit(solution)/shard_map/ppermute | solution.py:25
  52.3 65.1 %collective-permute-start.4 = (f32[4,5,16,2,16]{4,2,3,1,0:T(8,128)}, f32[4,5,16,2,16]{4,2,3,1,0:T(8,128)}, u32[]{:S(2)}, u32[]{:S(2)}) collective-permute-start(f32[4,5,16,2,16]{4,2,3,1,0:T(8,128)} %broadcast_select_fusion.1), channel_id=1, source_target_pairs={{0,31},{1,0},{2,1},{3,2},{4,3},{5,4},{6,5},{7,6},{8,7},{9,8},{10,9... | collective-permute-start | bytes 122888 | tf_op jit(solution)/shard_map/ppermute | solution.py:25
  59.2 60.9 %collective-permute-start.5 = (f32[4,5,16,2,16]{4,2,3,1,0:T(8,128)}, f32[4,5,16,2,16]{4,2,3,1,0:T(8,128)}, u32[]{:S(2)}, u32[]{:S(2)}) collective-permute-start(f32[4,5,16,2,16]{4,2,3,1,0:T(8,128)} %broadcast_select_fusion), channel_id=1, source_target_pairs={{0,30},{1,31},{2,0},{3,1},{4,2},{5,3},{6,4},{7,5},{8,6},{9,7},{10,... | collective-permute-start | bytes 122888 | tf_op jit(solution)/shard_map/ppermute | solution.py:25
  127.7 1.2 copy-start.2
  131.3 1.0 copy-start.6
  131.3 1.5 copy-start.5
  131.4 0.8 copy-start
  137.8 0.9 copy-start.4
  139.9 1.1 copy-start.1
  140.9 1.8 %copy-start.3 = (f32[3,6,5,16,2,16]{5,3,4,2,1,0:T(8,128)S(1)}, f32[3,6,5,16,2,16]{5,3,4,2,1,0:T(8,128)}, u32[]{:S(2)}) copy-start(f32[3,6,5,16,2,16]{5,3,4,2,1,0:T(8,128)} %copy-done.2) | copy-start | bytes 552964 | tf_op jit(solution)/shard_map/while
  142.7 1.2 copy-start.2
  146.3 1.0 copy-start.6
  146.3 1.5 copy-start.5
  146.5 0.8 copy-start
  152.8 0.9 copy-start.4
  154.9 1.1 copy-start.1
  156.0 1.8 %copy-start.3 = (f32[3,6,5,16,2,16]{5,3,4,2,1,0:T(8,128)S(1)}, f32[3,6,5,16,2,16]{5,3,4,2,1,0:T(8,128)}, u32[]{:S(2)}) copy-start(f32[3,6,5,16,2,16]{5,3,4,2,1,0:T(8,128)} %copy-done.2) | copy-start | bytes 552964 | tf_op jit(solution)/shard_map/while
  157.8 1.2 copy-start.2
  161.4 1.0 copy-start.6
  161.4 1.5 copy-start.5
  161.5 0.8 copy-start
  167.9 0.9 copy-start.4
  170.0 1.1 copy-start.1
  171.1 1.8 %copy-start.3 = (f32[3,6,5,16,2,16]{5,3,4,2,1,0:T(8,128)S(1)}, f32[3,6,5,16,2,16]{5,3,4,2,1,0:T(8,128)}, u32[]{:S(2)}) copy-start(f32[3,6,5,16,2,16]{5,3,4,2,1,0:T(8,128)} %copy-done.2) | copy-start | bytes 552964 | tf_op jit(solution)/shard_map/while
where the time goes:
time: 177 us; the launch traced here: 176 us
  local copies, waits for them, and re-layouts  60.6 us (34%)
  blocking collectives  49.2 us (28%)
  other arithmetic  48.4 us (27%)
  starting transfers between devices  13.6 us (8%)
    pmax x1, blocking collectives, body(): fastest_speed = lax.pmax(fastest(box_cells, occupied), ('curve', 'sub'))  49.2 us
    gather x4, local copies, waits for them, and re-layouts, unpack(): delivered = jnp.take(incoming, jnp.clip(recv_rank, 0, CAPG - 1), axis=0)  11 us
    unnamed x9, local copies, waits for them, and re-layouts  9.64 us
    sub x18, other arithmetic, flux_sweep(): 0.5 * (flux_left[field_index] + flux_right[field_index])  7.81 us
    ppermute x4, starting transfers between devices, passed_along_2(): return lax.ppermute(value, axis, pairs)  7.36 us
    select_n x8, other arithmetic, pack_for(): return jnp.take(strips, row_index, axis=0)  7.28 us
    ppermute x2, starting transfers between devices, passed_along(): return lax.ppermute(block, axis, route)  6.22 us
    while x42, local copies, waits for them, and re-layouts  5.71 us
  transfers between devices with their start and end apart: 6, of which 1 were waited for; matrix products, arithmetic and copies ran while one was open for 18% of the time, Pallas kernels for 0%

commit v1 on v0

v1 whole, which is shorter than its diff:
```python
import functools

import jax
import jax.numpy as jnp
from jax import lax
from jax.experimental import pallas as pl
from jax.experimental.pallas import tpu as pltpu
from jax.sharding import PartitionSpec as P

MESH = pl.DeviceIdType.MESH
SHIFTS = (1, -1, 2, -2)
CAPG = 4
SIDES = (1, 0, 3, 2, 5, 4)
GAMMA = 5.0 / 3.0
COURANT = 0.3
FILLER = (1.0, 0.0, 0.0, 0.0, 1.5)
VMEM = pl.BlockSpec(memory_space=pltpu.VMEM)
SMEM = pl.BlockSpec(memory_space=pltpu.SMEM)


def iota(shape, dim):
    return lax.broadcasted_iota(jnp.int32, shape, dim)


def dot(a, b):
    return jnp.dot(a, b, precision=lax.Precision.HIGHEST, preferred_element_type=jnp.float32)


def repeated(value):
    value = value + pltpu.roll(value, 64, 1)
    return value + pltpu.roll(value, 32, 1)


def primitives(state):
    inverse = 1.0 / state[0]
    vel = [state[k] * inverse for k in (1, 2, 3)]
    kinetic = 0.5 * state[0] * (vel[0] * vel[0] + vel[1] * vel[1] + vel[2] * vel[2])
    return [state[0], *vel, (GAMMA - 1.0) * (state[4] - kinetic)]


def exchange_kernel(
    sizes, fields, new_source, ghost, moved, packed, top,
    strips, move_out, move_in, face_out, face_in, top_out, top_in, top_out2, top_in2,
    move_sems, face_sems, top_sems, top_sems2,
):
    curves, subs = sizes
    count = curves * subs
    slots = fields.shape[0]
    curve, sub = lax.axis_index("curve"), lax.axis_index("sub")
    here = curve * subs + sub

    def at(shift):
        other = lax.rem(here + shift + count, count)
        return (other // subs, lax.rem(other, subs))

    sub_peers = [(curve, lax.rem(sub + k, subs)) for k in range(1, subs)]
    curve_peers = [(lax.rem(curve + k, curves), sub) for k in range(1, curves)]
    barrier = pltpu.get_barrier_semaphore()
    peers = sub_peers + curve_peers + [at(s) for s in SHIFTS]
    for peer in peers:
        pl.semaphore_signal(barrier, inc=1, device_id=peer, device_id_type=MESH)

    base = here * slots
    for n, shift in enumerate((1, -1)):
        receiver = lax.rem(here + shift + count, count)
        pick = jnp.int32(0)
        for j in range(slots):
            source = new_source[receiver * slots + j] - base
            pick = jnp.where((source >= 0) & (source < slots), source, pick)
        move_out[n] = fields[pick]

    around = [
        new_source[lax.rem(here + s + count, count) * slots + j]
        for s in (-1, 0, 1)
        for j in range(slots)
    ]
    fastest = jnp.zeros((8, 128), jnp.float32)
    for b in range(slots):
        used = jnp.int32(0)
        for source in around:
            used = jnp.where(source == base + b, 1, used)
        prim = primitives([fields[b, k] for k in range(5)])
        quick = jnp.maximum(jnp.maximum(jnp.abs(prim[1]), jnp.abs(prim[2])), jnp.abs(prim[3]))
        quick = quick + jnp.sqrt(GAMMA * prim[4] / prim[0])
        quick = jnp.where(used > 0, quick, 0.0)
        for r in (0, 8):
            for c in (0, 128):
                fastest = jnp.maximum(fastest, quick[r : r + 8, c : c + 128])
    top_out[...] = fastest

    pl.semaphore_wait(barrier, len(peers))

    moves = []
    for n, shift in enumerate((1, -1)):
        moves.append(
            pltpu.make_async_remote_copy(
                move_out.at[n], move_in.at[n], move_sems.at[0, n], move_sems.at[1, n],
                device_id=at(shift), device_id_type=MESH,
            )
        )
        moves[-1].start()
    firsts = []
    for n, peer in enumerate(sub_peers):
        firsts.append(
            pltpu.make_async_remote_copy(
                top_out, top_in.at[n], top_sems.at[0, n], top_sems.at[1, n],
                device_id=peer, device_id_type=MESH,
            )
        )
        firsts[-1].start()

    picks = []
    for shift in (0,) + SHIFTS:
        receiver = lax.rem(here + shift + count, count)
        rank = jnp.int32(0)
        chosen = [jnp.int32(0)] * CAPG
        for j in range(slots):
            for f in range(6):
                source = ghost[f, receiver * slots + j] - base
                going = (source >= 0) & (source < slots)
                row = source * 6 + SIDES[f]
                for k in range(CAPG):
                    chosen[k] = jnp.where(going & (rank == k), row, chosen[k])
                rank = rank + jnp.where(going, 1, 0)
        picks.append(chosen)

    own = [new_source[base + j] for j in range(slots)]
    for copy in firsts:
        copy.wait()
    fastest = top_out[...]
    for n in range(subs - 1):
        fastest = jnp.maximum(fastest, top_in[n])
    top_out2[...] = fastest
    seconds = []
    for n, peer in enumerate(curve_peers):
        seconds.append(
            pltpu.make_async_remote_copy(
                top_out2, top_in2.at[n], top_sems2.at[0, n], top_sems2.at[1, n],
                device_id=peer, device_id_type=MESH,
            )
        )
        seconds[-1].start()

    cell, column = iota((256, 256), 0), iota((256, 256), 1)
    inside = lax.rem(column, 32)
    wanted_cell = (inside // 2) * 16 + lax.rem(inside, 2) + jnp.where(column >= 128, 14, 0)
    x_picker = jnp.where(cell == wanted_cell, 1.0, 0.0)
    lane16 = iota((16, 128), 1)
    lane8, row8 = iota((8, 128), 1), iota((8, 128), 0)
    group_here = (lane8 // 32) == lax.rem(row8, 4)

    for copy in moves:
        copy.wait()
    for j in range(slots):
        source = own[j] - base
        local = (source >= 0) & (source < slots)
        slot = jnp.where(local, source, 0)
        for k in range(5):
            value = jnp.where(source < 0, move_in[0, k], move_in[1, k])
            value = jnp.where(local, fields[slot, k], value)
            moved[j, k] = jnp.where(own[j] >= 0, value, FILLER[k])
        for k in range(5):
            box = moved[j, k]
            x_strips = dot(box, x_picker)
            strips[j * 6 + 0, k] = x_strips[:, :128]
            strips[j * 6 + 1, k] = x_strips[:, 128:]
            strips[j * 6 + 2, k] = repeated(jnp.where(lane16 < 32, box[:, :128], 0.0))
            strips[j * 6 + 3, k] = repeated(jnp.where(lane16 >= 96, box[:, 128:], 0.0))
            for side, first in ((4, 0), (5, 14)):
                for layer in range(2):
                    line = box[first + layer : first + layer + 1]
                    spread = jnp.where(
                        row8 < 4,
                        jnp.broadcast_to(line[:, :128], (8, 128)),
                        jnp.broadcast_to(line[:, 128:], (8, 128)),
                    )
                    strips[j * 6 + side, k, pl.ds(layer * 8, 8)] = repeated(
                        jnp.where(group_here, spread, 0.0)
                    )

    group = iota((5, 16, 128), 2) // 32

    def gathered(chosen):
        value = strips[chosen[0]]
        for k in range(1, CAPG):
            value = jnp.where(group == k, strips[chosen[k]], value)
        return value

    faces = []
    for n, shift in enumerate(SHIFTS):
        face_out[n] = gathered(picks[n + 1])
        faces.append(
            pltpu.make_async_remote_copy(
                face_out.at[n], face_in.at[n], face_sems.at[0, n], face_sems.at[1, n],
                device_id=at(shift), device_id_type=MESH,
            )
        )
        faces[-1].start()
    packed[0] = gathered(picks[0])
    for copy in seconds:
        copy.wait()
    fastest = top_out2[...]
    for n in range(curves - 1):
        fastest = jnp.maximum(fastest, top_in2[n])
    top[...] = fastest
    for n, copy in enumerate(faces):
        copy.wait()
        packed[n + 1] = face_in[n]


def earlier(pair, axis):
    if axis == 0:
        edge = iota((16, 256), 1) % 16 == 0
        near = [pltpu.roll(v, 1, 1) for v in pair]
        far = [pltpu.roll(v, 241, 1) for v in pair]
    elif axis == 1:
        edge = iota((16, 256), 1) < 16
        near = far = [pltpu.roll(v, 16, 1) for v in pair]
    else:
        edge = iota((16, 256), 0) == 0
        near = far = [pltpu.roll(v, 1, 0) for v in pair]
    return jnp.where(edge, far[1], near[0]), jnp.where(edge, far[0], near[1])


def later(pair, axis, both=True):
    if axis == 0:
        edge = iota((16, 256), 1) % 16 == 15
        near = [pltpu.roll(v, 255, 1) for v in pair]
        far = [pltpu.roll(v, 15, 1) for v in pair]
    elif axis == 1:
        edge = iota((16, 256), 1) >= 240
        near = far = [pltpu.roll(v, 240, 1) for v in pair]
    else:
        edge = iota((16, 256), 0) == 15
        near = far = [pltpu.roll(v, 15, 0) for v in pair]
    first = jnp.where(edge, far[1], near[0])
    if not both:
        return first
    return first, jnp.where(edge, far[0], near[1])


def euler_terms(prim, axis):
    density, vel, pressure = prim[0], prim[1:4], prim[4]
    along = vel[axis]
    energy = pressure * (1.0 / (GAMMA - 1.0)) + 0.5 * density * (
        vel[0] * vel[0] + vel[1] * vel[1] + vel[2] * vel[2]
    )
    conserved = [density, density * vel[0], density * vel[1], density * vel[2], energy]
    fluxes = [value * along for value in conserved]
    fluxes[axis + 1] = fluxes[axis + 1] + pressure
    fluxes[4] = fluxes[4] + pressure * along
    return conserved, fluxes, jnp.abs(along) + jnp.sqrt(GAMMA * pressure / density)


def face_flux(left, right, axis):
    cons_l, flux_l, speed_l = euler_terms(left, axis)
    cons_r, flux_r, speed_r = euler_terms(right, axis)
    speed = jnp.maximum(speed_l, speed_r)
    return [0.5 * (flux_l[k] + flux_r[k]) - 0.5 * speed * (cons_r[k] - cons_l[k]) for k in range(5)]


def sweep(prim, prim_ghost, axis):
    lefts, rights = ([], []), ([], [])
    for k in range(5):
        pair = (prim[k], prim_ghost[k])
        before = earlier(pair, axis)
        step = (pair[0] - before[0], pair[1] - before[1])
        after = later(step, axis)
        ends = []
        for i in range(2):
            slope = jnp.maximum(0.0, jnp.minimum(step[i], after[i])) + jnp.minimum(
                0.0, jnp.maximum(step[i], after[i])
            )
            ends.append(pair[i] + 0.5 * slope)
            rights[i].append(pair[i] - 0.5 * slope)
        before = earlier(ends, axis)
        lefts[0].append(before[0])
        lefts[1].append(before[1])
    inner = face_flux(lefts[0], rights[0], axis)
    outer = face_flux(lefts[1], rights[1], axis)
    return [later((inner[k], outer[k]), axis, False) - inner[k] for k in range(5)]


def advance_kernel(sizes, moved, packed, top, new_source, ghost, out, where_from):
    curves, subs = sizes
    count = curves * subs
    slots = moved.shape[0]
    here = lax.axis_index("curve") * subs + lax.axis_index("sub")
    base = here * slots
    ranks = [jnp.int32(0)] * 5
    for j in range(slots):
        for f in range(6):
            source = ghost[f, base + j]
            row, group = jnp.int32(0), jnp.int32(-1)
            for n, shift in enumerate((0,) + SHIFTS):
                offset = source - lax.rem(here - shift + count, count) * slots
                hit = (offset >= 0) & (offset < slots)
                row = jnp.where(hit, n, row)
                group = jnp.where(hit, ranks[n], group)
                ranks[n] = ranks[n] + jnp.where(hit, 1, 0)
            where_from[0, j * 6 + f] = row
            where_from[1, j * 6 + f] = group
    ratio = COURANT / jnp.max(top[...])
    row_in, column = iota((256, 256), 0), iota((256, 256), 1)
    x = column % 16
    low_cell = (column // 16) * 2 + x - 14
    high_cell = 128 + (column // 16) * 2 + x
    x_spread = jnp.where(
        ((x >= 14) & (row_in == low_cell)) | ((x < 2) & (row_in == high_cell)), 1.0, 0.0
    )
    lane, row16 = iota((16, 128), 1), iota((16, 128), 0)
    row_wide = iota((16, 256), 0)

    @pl.loop(0, slots)
    def _(j):
        def strip(f, k):
            group = where_from[1, j * 6 + f]
            value = packed[where_from[0, j * 6 + f], k]
            value = repeated(jnp.where(lane // 32 == group, value, 0.0))
            return jnp.where(group >= 0, value, FILLER[k])

        def z_lines(f, k):
            value = jnp.where(lane // 32 == row16 % 4, strip(f, k), 0.0)
            sums = [jnp.sum(value[4 * i : 4 * i + 4], axis=0, keepdims=True) for i in range(4)]
            return [jnp.concatenate(sums[2 * i : 2 * i + 2], axis=1) for i in range(2)]

        box = [moved[j, k] for k in range(5)]
        prim = primitives(box)
        total = None
        for axis in range(3):
            ghosts = []
            for k in range(5):
                if axis < 2:
                    low, high = strip(2 * axis, k), strip(2 * axis + 1, k)
                if axis == 0:
                    ghosts.append(dot(jnp.concatenate([low, high], axis=1), x_spread))
                elif axis == 1:
                    ghosts.append(jnp.concatenate([high, low], axis=1))
                else:
                    low, high = z_lines(4, k), z_lines(5, k)
                    value = jnp.where(row_wide == 14, low[0], low[1])
                    value = jnp.where(row_wide == 1, high[1], value)
                    ghosts.append(jnp.where(row_wide == 0, high[0], value))
            change = sweep(prim, primitives(ghosts), axis)
            total = change if total is None else [a + b for a, b in zip(total, change)]
        taken = new_source[base + j] >= 0
        for k in range(5):
            out[j, k] = jnp.where(taken, box[k] - ratio * total[k], 0.0)


def body(sizes, fields, new_source, ghost_source):
    curves, subs = sizes
    slots = fields.shape[0]
    ghost = ghost_source.T
    f32 = jnp.float32
    tile = (5, 16, 128)
    moved, packed, top = pl.pallas_call(
        functools.partial(exchange_kernel, sizes),
        out_shape=[
            jax.ShapeDtypeStruct(fields.shape, f32),
            jax.ShapeDtypeStruct((5,) + tile, f32),
            jax.ShapeDtypeStruct((8, 128), f32),
        ],
        in_specs=[VMEM, SMEM, SMEM],
        out_specs=[VMEM] * 3,
        scratch_shapes=[
            pltpu.VMEM((slots * 6,) + tile, f32),
            pltpu.VMEM((2,) + fields.shape[1:], f32),
            pltpu.VMEM((2,) + fields.shape[1:], f32),
            pltpu.VMEM((4,) + tile, f32),
            pltpu.VMEM((4,) + tile, f32),
            pltpu.VMEM((8, 128), f32),
            pltpu.VMEM((subs - 1, 8, 128), f32),
            pltpu.VMEM((8, 128), f32),
            pltpu.VMEM((curves - 1, 8, 128), f32),
            pltpu.SemaphoreType.DMA((2, 2)),
            pltpu.SemaphoreType.DMA((2, 4)),
            pltpu.SemaphoreType.DMA((2, subs - 1)),
            pltpu.SemaphoreType.DMA((2, curves - 1)),
        ],
        compiler_params=pltpu.CompilerParams(
            collective_id=0, has_side_effects=True, vmem_limit_bytes=24 << 20
        ),
    )(fields, new_source, ghost)
    return pl.pallas_call(
        functools.partial(advance_kernel, sizes),
        out_shape=jax.ShapeDtypeStruct(fields.shape, f32),
        in_specs=[VMEM, VMEM, VMEM, SMEM, SMEM],
        out_specs=VMEM,
        scratch_shapes=[pltpu.SMEM((2, slots * 6), jnp.int32)],
        compiler_params=pltpu.CompilerParams(vmem_limit_bytes=24 << 20),
    )(moved, packed, top, new_source, ghost)


def solution(mesh):
    placed = P(("curve", "sub"), None, None, None)
    sizes = (mesh.shape["curve"], mesh.shape["sub"])
    return jax.shard_map(
        functools.partial(body, sizes),
        mesh=mesh,
        in_specs=(placed, P(), P()),
        out_specs=placed,
        check_vma=False,
    )
```

time: 177 us -> 29.5 us (0.17)
  local copies, waits for them, and re-layouts: 60.6 us -> 2.28 us
  blocking collectives: 49.2 us -> 0 us
  other arithmetic: 48.4 us -> 0 us
  Pallas kernels: 0 us -> 27 us
  starting transfers between devices: 13.6 us -> 0 us
    pmax x1 -> x0, blocking collectives: 49.2 us -> none  [body(): fastest_speed = lax.pmax(fastest(box_cells, occupied), ('curve', 'sub'))]
    pallas_call x0 -> x2, Pallas kernels: none -> 27 us  [the longest x1 19.8 us: body(): pl.pallas_call(functools.partial(exchange_kernel, sizes), out_shape=[jax....]
    gather x11 -> x0, local copies, waits for them, and re-layouts: 20.5 us -> none  [the longest x4 11 us: unpack(): delivered = jnp.take(incoming, jnp.clip(recv_rank, 0, CAPG - 1), axis=0)]
    select_n x15 -> x0, other arithmetic: 14.1 us -> none  [the longest x8 7.28 us: pack_for(): return jnp.take(strips, row_index, axis=0)]
    ppermute x6 -> x0, starting transfers between devices: 13.6 us -> none  [the longest x4 7.36 us: passed_along_2(): return lax.ppermute(value, axis, pairs)]
    sub x49 -> x0, other arithmetic: 9.88 us -> none  [the longest x18 7.81 us: flux_sweep(): 0.5 * (flux_left[field_index] + flux_right[field_index])]
    unnamed x9 -> x6, local copies, waits for them, and re-layouts: 9.64 us -> 2.28 us
    concatenate x10 -> x0, other arithmetic: 6.22 us -> none  [the longest x3 4.47 us: advance(): jnp.concatenate([jnp.swapaxes(ghosts[:, 0], -1, -2), box_cells, jnp.swapa...]
  transfers between devices with their start and end apart: 6 -> 0, of which waited for: 1 -> 0; matrix products, arithmetic and copies ran while one was open for 18% -> 0% of each run, Pallas kernels for 0% -> 0%
where the time goes in v1:
time: 29.5 us; the launch traced here: 29.3 us
  Pallas kernels  27 us (92%)
  local copies, waits for them, and re-layouts  2.28 us (8%)
    pallas_call x1, Pallas kernels, body(): pl.pallas_call(functools.partial(exchange_kernel, sizes), out_shape=[jax....  19.8 us
    pallas_call x1, Pallas kernels, body(): pl.pallas_call(functools.partial(advance_kernel, sizes), out_shape=jax.Sh...  7.26 us
    unnamed x6, local copies, waits for them, and re-layouts  2.28 us

profile of v1, /device:TPU:0, one launch (start us, length us, event | category | flops | bytes accessed | tf_op | source)
XLA Modules:
  0.0 29.3 jit_solution(2324624882433081682)
XLA Ops:
  0.0 0.0 copy-start.2
  0.0 0.7 %copy-done.2 = s32[96]{0:T(128)S(1)} copy-done((s32[96]{0:T(128)S(1)}, s32[96]{0:T(128)}, u32[]{:S(2)}) %copy-start.2) | copy-done | bytes 408
  0.7 0.0 copy-start
  0.7 0.9 %copy-done = f32[3,5,16,256]{3,2,1,0:T(8,128)S(1)} copy-done((f32[3,5,16,256]{3,2,1,0:T(8,128)S(1)}, f32[3,5,16,256]{3,2,1,0:T(8,128)}, u32[]{:S(2)}) %copy-start) | copy-done | bytes 245784
  1.6 0.0 copy-start.1
  1.6 0.7 %copy-done.1 = s32[96,6]{0,1:T(8,128)S(1)} copy-done((s32[96,6]{0,1:T(8,128)S(1)}, s32[96,6]{0,1:T(8,128)}, u32[]{:S(2)}) %copy-start.1) | copy-done | bytes 2328
  2.3 19.8 %shard_map.37 = (f32[3,5,16,256]{3,2,1,0:T(8,128)S(1)}, f32[5,5,16,128]{3,2,1,0:T(8,128)S(1)}, f32[8,128]{1,0:T(8,128)S(1)}) custom-call(f32[3,5,16,256]{3,2,1,0:T(8,128)S(1)} %copy-done, s32[96]{0:T(128)S(1)} %copy-done.2, s32[6,96]{1,0:T(8,128)S(1)} %bitcast.1), custom_call_target="tpu_custom_call" | custom-call | tf_op jit(solution)/shard_map/pallas_call | solution.py:357
  22.1 7.3 %shard_map.38 = f32[3,5,16,256]{3,2,1,0:T(8,128)} custom-call(f32[3,5,16,256]{3,2,1,0:T(8,128)S(1)} %get-tuple-element.8.moved, f32[5,5,16,128]{3,2,1,0:T(8,128)S(1)} %get-tuple-element.9.packed, f32[8,128]{1,0:T(8,128)S(1)} %get-tuple-element.10.top, s32[96]{0:T(128)S(1)} %copy-done.2, s32[6,96]{1,0:T(8,128)S(1)} %bitcast.2), custom_call_target="tpu_custom_call" | custom-call | tf_op jit(solution)/shard_map/pallas_call | solution.py:385
Async XLA Ops:
  0.0 0.7 %copy-start.2 = (s32[96]{0:T(128)S(1)}, s32[96]{0:T(128)}, u32[]{:S(2)}) copy-start(s32[96]{0:T(128)} %new_source.3) | copy-start | bytes 1156
  0.7 0.9 %copy-start = (f32[3,5,16,256]{3,2,1,0:T(8,128)S(1)}, f32[3,5,16,256]{3,2,1,0:T(8,128)}, u32[]{:S(2)}) copy-start(f32[3,5,16,256]{3,2,1,0:T(8,128)} %fields.1) | copy-start | bytes 737284
  1.6 0.7 %copy-start.1 = (s32[96,6]{0,1:T(8,128)S(1)}, s32[96,6]{0,1:T(8,128)}, u32[]{:S(2)}) copy-start(s32[96,6]{0,1:T(8,128)} %param.5) | copy-start | bytes 6916

commit v2 on v1

--- a/solution.py
+++ b/solution.py
@@ -22,8 +22,14 @@
     return lax.broadcasted_iota(jnp.int32, shape, dim)
 
 
-def dot(a, b):
-    return jnp.dot(a, b, precision=lax.Precision.HIGHEST, preferred_element_type=jnp.float32)
+def picked(values, one_hot):
+    rows = values.shape[0]
+    parts = []
+    for _ in range(3):
+        parts.append(values.astype(jnp.bfloat16))
+        values = values - parts[-1].astype(jnp.float32)
+    product = jnp.dot(jnp.concatenate(parts, axis=0), one_hot, preferred_element_type=jnp.float32)
+    return product[:rows] + product[rows : 2 * rows] + product[2 * rows :]
 
 
 def repeated(value):
@@ -39,13 +45,20 @@
 
 
 def exchange_kernel(
-    sizes, fields, new_source, ghost, moved, packed, top,
-    strips, move_out, move_in, face_out, face_in, top_out, top_in, top_out2, top_in2,
+    sizes, fields_hbm, new_source_hbm, ghost_hbm, moved, packed, top,
+    fields, new_source, ghost, load_sems, strips, move_out, move_in, face_out, face_in, top_out, top_in, top_out2, top_in2,
     move_sems, face_sems, top_sems, top_sems2,
 ):
     curves, subs = sizes
     count = curves * subs
     slots = fields.shape[0]
+    loads = [
+        pltpu.make_async_copy(new_source_hbm, new_source, load_sems.at[0]),
+        pltpu.make_async_copy(fields_hbm, fields, load_sems.at[1]),
+        pltpu.make_async_copy(ghost_hbm, ghost, load_sems.at[2]),
+    ]
+    for copy in loads:
+        copy.start()
     curve, sub = lax.axis_index("curve"), lax.axis_index("sub")
     here = curve * subs + sub
 
@@ -60,6 +73,8 @@
     for peer in peers:
         pl.semaphore_signal(barrier, inc=1, device_id=peer, device_id_type=MESH)
 
+    loads[0].wait()
+    loads[1].wait()
     base = here * slots
     for n, shift in enumerate((1, -1)):
         receiver = lax.rem(here + shift + count, count)
@@ -90,15 +105,6 @@
 
     pl.semaphore_wait(barrier, len(peers))
 
-    moves = []
-    for n, shift in enumerate((1, -1)):
-        moves.append(
-            pltpu.make_async_remote_copy(
-                move_out.at[n], move_in.at[n], move_sems.at[0, n], move_sems.at[1, n],
-                device_id=at(shift), device_id_type=MESH,
-            )
-        )
-        moves[-1].start()
     firsts = []
     for n, peer in enumerate(sub_peers):
         firsts.append(
@@ -108,7 +114,19 @@
             )
         )
         firsts[-1].start()
-
+    moves = []
+    for k in range(5):
+        for n, shift in enumerate((1, -1)):
+            moves.append(
+                pltpu.make_async_remote_copy(
+                    move_out.at[n, k], move_in.at[n, k],
+                    move_sems.at[0, n, k], move_sems.at[1, n, k],
+                    device_id=at(shift), device_id_type=MESH,
+                )
+            )
+            moves[-1].start()
+
+    loads[2].wait()
     picks = []
     for shift in (0,) + SHIFTS:
         receiver = lax.rem(here + shift + count, count)
@@ -125,45 +143,57 @@
         picks.append(chosen)
 
     own = [new_source[base + j] for j in range(slots)]
-    for copy in firsts:
-        copy.wait()
-    fastest = top_out[...]
-    for n in range(subs - 1):
-        fastest = jnp.maximum(fastest, top_in[n])
-    top_out2[...] = fastest
-    seconds = []
-    for n, peer in enumerate(curve_peers):
-        seconds.append(
-            pltpu.make_async_remote_copy(
-                top_out2, top_in2.at[n], top_sems2.at[0, n], top_sems2.at[1, n],
-                device_id=peer, device_id_type=MESH,
-            )
-        )
-        seconds[-1].start()
-
     cell, column = iota((256, 256), 0), iota((256, 256), 1)
     inside = lax.rem(column, 32)
     wanted_cell = (inside // 2) * 16 + lax.rem(inside, 2) + jnp.where(column >= 128, 14, 0)
-    x_picker = jnp.where(cell == wanted_cell, 1.0, 0.0)
+    x_picker = jnp.where(cell == wanted_cell, 1.0, 0.0).astype(jnp.bfloat16)
     lane16 = iota((16, 128), 1)
     lane8, row8 = iota((8, 128), 1), iota((8, 128), 0)
     group_here = (lane8 // 32) == lax.rem(row8, 4)
 
-    for copy in moves:
-        copy.wait()
-    for j in range(slots):
-        source = own[j] - base
-        local = (source >= 0) & (source < slots)
-        slot = jnp.where(local, source, 0)
-        for k in range(5):
+    group = iota((16, 128), 1) // 32
+
+    def gathered(chosen, k):
+        value = strips[chosen[0], k]
+        for i in range(1, CAPG):
+            value = jnp.where(group == i, strips[chosen[i], k], value)
+        return value
+
+    def second_stage():
+        for copy in firsts:
+            copy.wait()
+        fastest = top_out[...]
+        for n in range(subs - 1):
+            fastest = jnp.maximum(fastest, top_in[n])
+        top_out2[...] = fastest
+        copies = []
+        for n, peer in enumerate(curve_peers):
+            copies.append(
+                pltpu.make_async_remote_copy(
+                    top_out2, top_in2.at[n], top_sems2.at[0, n], top_sems2.at[1, n],
+                    device_id=peer, device_id_type=MESH,
+                )
+            )
+            copies[-1].start()
+        return copies
+
+    faces = []
+    for k in range(5):
+        moves[2 * k].wait()
+        moves[2 * k + 1].wait()
+        boxes = []
+        for j in range(slots):
+            source = own[j] - base
+            local = (source >= 0) & (source < slots)
+            slot = jnp.where(local, source, 0)
             value = jnp.where(source < 0, move_in[0, k], move_in[1, k])
             value = jnp.where(local, fields[slot, k], value)
-            moved[j, k] = jnp.where(own[j] >= 0, value, FILLER[k])
-        for k in range(5):
-            box = moved[j, k]
-            x_strips = dot(box, x_picker)
-            strips[j * 6 + 0, k] = x_strips[:, :128]
-            strips[j * 6 + 1, k] = x_strips[:, 128:]
+            boxes.append(jnp.where(own[j] >= 0, value, FILLER[k]))
+            moved[j, k] = boxes[j]
+        x_strips = picked(jnp.concatenate(boxes, axis=0), x_picker)
+        for j, box in enumerate(boxes):
+            strips[j * 6 + 0, k] = x_strips[j * 16 : j * 16 + 16, :128]
+            strips[j * 6 + 1, k] = x_strips[j * 16 : j * 16 + 16, 128:]
             strips[j * 6 + 2, k] = repeated(jnp.where(lane16 < 32, box[:, :128], 0.0))
             strips[j * 6 + 3, k] = repeated(jnp.where(lane16 >= 96, box[:, 128:], 0.0))
             for side, first in ((4, 0), (5, 14)):
@@ -177,66 +207,79 @@
                     strips[j * 6 + side, k, pl.ds(layer * 8, 8)] = repeated(
                         jnp.where(group_here, spread, 0.0)
                     )
-
-    group = iota((5, 16, 128), 2) // 32
-
-    def gathered(chosen):
-        value = strips[chosen[0]]
-        for k in range(1, CAPG):
-            value = jnp.where(group == k, strips[chosen[k]], value)
-        return value
-
-    faces = []
-    for n, shift in enumerate(SHIFTS):
-        face_out[n] = gathered(picks[n + 1])
-        faces.append(
-            pltpu.make_async_remote_copy(
-                face_out.at[n], face_in.at[n], face_sems.at[0, n], face_sems.at[1, n],
-                device_id=at(shift), device_id_type=MESH,
+        for n, shift in enumerate(SHIFTS):
+            face_out[n, k] = gathered(picks[n + 1], k)
+            faces.append(
+                pltpu.make_async_remote_copy(
+                    face_out.at[n, k], face_in.at[n, k],
+                    face_sems.at[0, n, k], face_sems.at[1, n, k],
+                    device_id=at(shift), device_id_type=MESH,
+                )
             )
-        )
-        faces[-1].start()
-    packed[0] = gathered(picks[0])
+            faces[-1].start()
+        packed[0, k] = gathered(picks[0], k)
+        if k == 0:
+            seconds = second_stage()
     for copy in seconds:
         copy.wait()
     fastest = top_out2[...]
     for n in range(curves - 1):
         fastest = jnp.maximum(fastest, top_in2[n])
     top[...] = fastest
-    for n, copy in enumerate(faces):
-        copy.wait()
-        packed[n + 1] = face_in[n]
+    for k in range(5):
+        for n in range(len(SHIFTS)):
+            faces[k * len(SHIFTS) + n].wait()
+            packed[n + 1, k] = face_in[n, k]
 
 
 def earlier(pair, axis):
+    box, ghost = pair
     if axis == 0:
         edge = iota((16, 256), 1) % 16 == 0
-        near = [pltpu.roll(v, 1, 1) for v in pair]
-        far = [pltpu.roll(v, 241, 1) for v in pair]
-    elif axis == 1:
-        edge = iota((16, 256), 1) < 16
-        near = far = [pltpu.roll(v, 16, 1) for v in pair]
-    else:
-        edge = iota((16, 256), 0) == 0
-        near = far = [pltpu.roll(v, 1, 0) for v in pair]
-    return jnp.where(edge, far[1], near[0]), jnp.where(edge, far[0], near[1])
-
-
-def later(pair, axis, both=True):
+        return (
+            jnp.where(edge, pltpu.roll(ghost, 241, 1), pltpu.roll(box, 1, 1)),
+            jnp.where(edge, pltpu.roll(box, 241, 1), pltpu.roll(ghost, 1, 1)),
+        )
+    if axis == 1:
+        box, ghost = pltpu.roll(box, 16, 1), pltpu.roll(ghost, 16, 1)
+        edge = iota((16, 128), 1) < 16
+        low = box[:, :128]
+        return (
+            jnp.concatenate([jnp.where(edge, ghost, low), box[:, 128:]], axis=1),
+            jnp.where(edge, low, ghost),
+        )
+    box, ghost = pltpu.roll(box, 1, 0), pltpu.roll(ghost, 1, 0)
+    edge = iota((8, 256), 0) == 0
+    low = box[:8]
+    return (
+        jnp.concatenate([jnp.where(edge, ghost, low), box[8:]], axis=0),
+        jnp.where(edge, low, ghost),
+    )
+
+
+def later(pair, axis):
+    box, ghost = pair
     if axis == 0:
         edge = iota((16, 256), 1) % 16 == 15
-        near = [pltpu.roll(v, 255, 1) for v in pair]
-        far = [pltpu.roll(v, 15, 1) for v in pair]
-    elif axis == 1:
-        edge = iota((16, 256), 1) >= 240
-        near = far = [pltpu.roll(v, 240, 1) for v in pair]
-    else:
-        edge = iota((16, 256), 0) == 15
-        near = far = [pltpu.roll(v, 15, 0) for v in pair]
-    first = jnp.where(edge, far[1], near[0])
-    if not both:
-        return first
-    return first, jnp.where(edge, far[0], near[1])
+        return (
+            jnp.where(edge, pltpu.roll(ghost, 15, 1), pltpu.roll(box, 255, 1)),
+            jnp.where(edge, pltpu.roll(box, 15, 1), pltpu.roll(ghost, 255, 1)),
+        )
+    if axis == 1:
+        box, ghost = pltpu.roll(box, 240, 1), pltpu.roll(ghost, 112, 1)
+        edge = iota((16, 128), 1) >= 112
+        high = box[:, 128:]
+        return (
+            jnp.concatenate([box[:, :128], jnp.where(edge, ghost, high)], axis=1),
+            jnp.where(edge, high, ghost),
+        )
+    box, ghost = pltpu.roll(box, 15, 0), pltpu.roll(ghost, 7, 0)
+    edge = iota((8, 256), 0) == 7
+    high = box[8:]
+    return (
+        jnp.concatenate([box[:8], jnp.where(edge, ghost, high)], axis=0),
+        jnp.where(edge, high, ghost),
+    )
 
 
 def euler_terms(prim, axis):
@@ -278,7 +321,7 @@
         lefts[1].append(before[1])
     inner = face_flux(lefts[0], rights[0], axis)
     outer = face_flux(lefts[1], rights[1], axis)
-    return [later((inner[k], outer[k]), axis, False) - inner[k] for k in range(5)]
+    return [later((inner[k], outer[k]), axis)[0] - inner[k] for k in range(5)]
 
 
 def advance_kernel(sizes, moved, packed, top, new_source, ghost, out, where_from):
@@ -307,9 +350,9 @@
     high_cell = 128 + (column // 16) * 2 + x
     x_spread = jnp.where(
         ((x >= 14) & (row_in == low_cell)) | ((x < 2) & (row_in == high_cell)), 1.0, 0.0
-    )
+    ).astype(jnp.bfloat16)
     lane, row16 = iota((16, 128), 1), iota((16, 128), 0)
-    row_wide = iota((16, 256), 0)
+    row_wide = iota((8, 256), 0)
 
     @pl.loop(0, slots)
     def _(j):
@@ -328,19 +371,22 @@
         prim = primitives(box)
         total = None
         for axis in range(3):
-            ghosts = []
+            ghosts, sides = [], []
             for k in range(5):
                 if axis < 2:
                     low, high = strip(2 * axis, k), strip(2 * axis + 1, k)
                 if axis == 0:
-                    ghosts.append(dot(jnp.concatenate([low, high], axis=1), x_spread))
+                    sides.append(jnp.concatenate([low, high], axis=1))
                 elif axis == 1:
-                    ghosts.append(jnp.concatenate([high, low], axis=1))
+                    ghosts.append(jnp.where(lane < 64, high, low))
                 else:
                     low, high = z_lines(4, k), z_lines(5, k)
-                    value = jnp.where(row_wide == 14, low[0], low[1])
+                    value = jnp.where(row_wide == 6, low[0], low[1])
                     value = jnp.where(row_wide == 1, high[1], value)
                     ghosts.append(jnp.where(row_wide == 0, high[0], value))
+            if axis == 0:
+                spread = picked(jnp.concatenate(sides, axis=0), x_spread)
+                ghosts = [spread[16 * k : 16 * k + 16] for k in range(5)]
             change = sweep(prim, primitives(ghosts), axis)
             total = change if total is None else [a + b for a, b in zip(total, change)]
         taken = new_source[base + j] >= 0
@@ -361,9 +407,13 @@
             jax.ShapeDtypeStruct((5,) + tile, f32),
             jax.ShapeDtypeStruct((8, 128), f32),
         ],
-        in_specs=[VMEM, SMEM, SMEM],
+        in_specs=[pl.BlockSpec(memory_space=pltpu.HBM)] * 3,
         out_specs=[VMEM] * 3,
         scratch_shapes=[
+            pltpu.VMEM(fields.shape, f32),
+            pltpu.SMEM(new_source.shape, jnp.int32),
+            pltpu.SMEM(ghost.shape, jnp.int32),
+            pltpu.SemaphoreType.DMA((3,)),
             pltpu.VMEM((slots * 6,) + tile, f32),
             pltpu.VMEM((2,) + fields.shape[1:], f32),
             pltpu.VMEM((2,) + fields.shape[1:], f32),
@@ -373,8 +423,8 @@
             pltpu.VMEM((subs - 1, 8, 128), f32),
             pltpu.VMEM((8, 128), f32),
             pltpu.VMEM((curves - 1, 8, 128), f32),
-            pltpu.SemaphoreType.DMA((2, 2)),
-            pltpu.SemaphoreType.DMA((2, 4)),
+            pltpu.SemaphoreType.DMA((2, 2, 5)),
+            pltpu.SemaphoreType.DMA((2, 4, 5)),
             pltpu.SemaphoreType.DMA((2, subs - 1)),
             pltpu.SemaphoreType.DMA((2, curves - 1)),
         ],

time: 29.5 us -> 26.1 us (0.88)
  Pallas kernels: 27 us -> 23.6 us
    pallas_call x1, Pallas kernels: 7.26 us -> 4.87 us  [body(): pl.pallas_call(functools.partial(advance_kernel, sizes), out_shape=jax.Sh...]
    pallas_call x1, Pallas kernels: 19.8 us -> 18.8 us  [body(): pl.pallas_call(functools.partial(exchange_kernel, sizes), out_shape=[jax....]
where the time goes in v2:
time: 26.1 us; the launch traced here: 25.9 us
  Pallas kernels  23.6 us (90%)
  local copies, waits for them, and re-layouts  2.28 us (9%)
    pallas_call x1, Pallas kernels, body(): pl.pallas_call(functools.partial(exchange_kernel, sizes), out_shape=[jax....  18.8 us
    pallas_call x1, Pallas kernels, body(): pl.pallas_call(functools.partial(advance_kernel, sizes), out_shape=jax.Sh...  4.87 us
    unnamed x6, local copies, waits for them, and re-layouts  2.28 us

profile of v2, /device:TPU:0, one launch (start us, length us, event | category | flops | bytes accessed | tf_op | source)
XLA Modules:
  0.0 25.9 jit_solution(15721274559420283531)
XLA Ops:
  0.0 0.0 copy-start.2
  0.0 0.7 %copy-done.2 = s32[96]{0:T(128)S(1)} copy-done((s32[96]{0:T(128)S(1)}, s32[96]{0:T(128)}, u32[]{:S(2)}) %copy-start.2) | copy-done | bytes 408
  0.7 0.0 copy-start
  0.7 0.9 %copy-done = f32[3,5,16,256]{3,2,1,0:T(8,128)S(1)} copy-done((f32[3,5,16,256]{3,2,1,0:T(8,128)S(1)}, f32[3,5,16,256]{3,2,1,0:T(8,128)}, u32[]{:S(2)}) %copy-start) | copy-done | bytes 245784
  1.6 0.0 copy-start.1
  1.6 0.7 %copy-done.1 = s32[96,6]{0,1:T(8,128)S(1)} copy-done((s32[96,6]{0,1:T(8,128)S(1)}, s32[96,6]{0,1:T(8,128)}, u32[]{:S(2)}) %copy-start.1) | copy-done | bytes 2328
  2.3 18.8 %shard_map.37 = (f32[3,5,16,256]{3,2,1,0:T(8,128)S(1)}, f32[5,5,16,128]{3,2,1,0:T(8,128)S(1)}, f32[8,128]{1,0:T(8,128)S(1)}) custom-call(f32[3,5,16,256]{3,2,1,0:T(8,128)S(1)} %copy-done, s32[96]{0:T(128)S(1)} %copy-done.2, s32[6,96]{1,0:T(8,128)S(1)} %bitcast.1), custom_call_target="tpu_custom_call" | custom-call | tf_op jit(solution)/shard_map/pallas_call | solution.py:403
  21.1 4.9 %shard_map.38 = f32[3,5,16,256]{3,2,1,0:T(8,128)} custom-call(f32[3,5,16,256]{3,2,1,0:T(8,128)S(1)} %get-tuple-element.8.moved, f32[5,5,16,128]{3,2,1,0:T(8,128)S(1)} %get-tuple-element.9.packed, f32[8,128]{1,0:T(8,128)S(1)} %get-tuple-element.10.top, s32[96]{0:T(128)S(1)} %copy-done.2, s32[6,96]{1,0:T(8,128)S(1)} %bitcast.2), custom_call_target="tpu_custom_call" | custom-call | tf_op jit(solution)/shard_map/pallas_call | solution.py:435
Async XLA Ops:
  0.0 0.7 %copy-start.2 = (s32[96]{0:T(128)S(1)}, s32[96]{0:T(128)}, u32[]{:S(2)}) copy-start(s32[96]{0:T(128)} %new_source.1) | copy-start | bytes 1156
  0.7 0.9 %copy-start = (f32[3,5,16,256]{3,2,1,0:T(8,128)S(1)}, f32[3,5,16,256]{3,2,1,0:T(8,128)}, u32[]{:S(2)}) copy-start(f32[3,5,16,256]{3,2,1,0:T(8,128)} %fields_hbm.1) | copy-start | bytes 737284
  1.6 0.7 %copy-start.1 = (s32[96,6]{0,1:T(8,128)S(1)}, s32[96,6]{0,1:T(8,128)}, u32[]{:S(2)}) copy-start(s32[96,6]{0,1:T(8,128)} %param.5) | copy-start | bytes 6916

commit v3 on v2

--- a/solution.py
+++ b/solution.py
@@ -15,7 +15,6 @@
 COURANT = 0.3
 FILLER = (1.0, 0.0, 0.0, 0.0, 1.5)
 VMEM = pl.BlockSpec(memory_space=pltpu.VMEM)
-SMEM = pl.BlockSpec(memory_space=pltpu.SMEM)
 
 
 def iota(shape, dim):
@@ -44,8 +43,50 @@
     return [state[0], *vel, (GAMMA - 1.0) * (state[4] - kinetic)]
 
 
-def exchange_kernel(
-    sizes, fields_hbm, new_source_hbm, ghost_hbm, moved, packed, top,
+def before(value, axis):
+    return pltpu.roll(value, (1, 16, 1)[axis], (1, 1, 0)[axis])
+
+
+def after(value, axis):
+    return pltpu.roll(value, (255, 240, 15)[axis], (1, 1, 0)[axis])
+
+
+def euler_terms(prim, axis):
+    density, vel, pressure = prim[0], prim[1:4], prim[4]
+    along = vel[axis]
+    energy = pressure * (1.0 / (GAMMA - 1.0)) + 0.5 * density * (
+        vel[0] * vel[0] + vel[1] * vel[1] + vel[2] * vel[2]
+    )
+    conserved = [density, density * vel[0], density * vel[1], density * vel[2], energy]
+    fluxes = [value * along for value in conserved]
+    fluxes[axis + 1] = fluxes[axis + 1] + pressure
+    fluxes[4] = fluxes[4] + pressure * along
+    return conserved, fluxes, jnp.abs(along) + jnp.sqrt(GAMMA * pressure / density)
+
+
+def face_flux(left, right, axis):
+    cons_l, flux_l, speed_l = euler_terms(left, axis)
+    cons_r, flux_r, speed_r = euler_terms(right, axis)
+    speed = jnp.maximum(speed_l, speed_r)
+    return [0.5 * (flux_l[k] + flux_r[k]) - 0.5 * speed * (cons_r[k] - cons_l[k]) for k in range(5)]
+
+
+def sweep(prim, axis):
+    lefts, rights = [], []
+    for value in prim:
+        step = value - before(value, axis)
+        ahead = after(step, axis)
+        slope = jnp.maximum(0.0, jnp.minimum(step, ahead)) + jnp.minimum(
+            0.0, jnp.maximum(step, ahead)
+        )
+        rights.append(value - 0.5 * slope)
+        lefts.append(before(value + 0.5 * slope, axis))
+    flux = face_flux(lefts, rights, axis)
+    return [after(value, axis) - value for value in flux]
+
+
+def step_kernel(
+    sizes, fields_hbm, new_source_hbm, ghost_hbm, out, moved, packed, partial, where_from,
     fields, new_source, ghost, load_sems, strips, move_out, move_in, face_out, face_in, top_out, top_in, top_out2, top_in2,
     move_sems, face_sems, top_sems, top_sems2,
 ):
@@ -142,6 +183,19 @@
                 rank = rank + jnp.where(going, 1, 0)
         picks.append(chosen)
 
+    ranks = [jnp.int32(0)] * 5
+    for j in range(slots):
+        for f in range(6):
+            source = ghost[f, base + j]
+            row, place = jnp.int32(0), jnp.int32(-1)
+            for n, shift in enumerate((0,) + SHIFTS):
+                offset = source - lax.rem(here - shift + count, count) * slots
+                hit = (offset >= 0) & (offset < slots)
+                row = jnp.where(hit, n, row)
+                place = jnp.where(hit, ranks[n], place)
+                ranks[n] = ranks[n] + jnp.where(hit, 1, 0)
+            where_from[0, j * 6 + f] = row
+            where_from[1, j * 6 + f] = place
     own = [new_source[base + j] for j in range(slots)]
     cell, column = iota((256, 256), 0), iota((256, 256), 1)
     inside = lax.rem(column, 32)
@@ -225,170 +279,93 @@
     fastest = top_out2[...]
     for n in range(curves - 1):
         fastest = jnp.maximum(fastest, top_in2[n])
-    top[...] = fastest
+    ratio = COURANT / jnp.max(fastest)
+
+    wide_lane, wide_row = iota((16, 256), 1), iota((16, 256), 0)
+    places = (lax.rem(wide_lane, 16), wide_lane // 16, wide_row)
+
+    @pl.loop(0, slots)
+    def _(j):
+        prim = primitives([moved[j, k] for k in range(5)])
+        total = [0.0] * 5
+        for axis in range(3):
+            inner = (places[axis] >= 2) & (places[axis] < 14)
+            change = sweep(prim, axis)
+            total = [total[k] + jnp.where(inner, change[k], 0.0) for k in range(5)]
+        for k in range(5):
+            partial[j, k] = total[k]
+
+    row_in, column = iota((256, 256), 0), iota((256, 256), 1)
+    x = lax.rem(column, 16)
+    low_cell = (column // 16) * 2 + x
+    high_cell = 128 + (column // 16) * 2 + x - 14
+    x_spread = jnp.where(
+        ((x < 2) & (row_in == low_cell)) | ((x >= 14) & (row_in == high_cell)), 1.0, 0.0
+    ).astype(jnp.bfloat16)
+    row16 = iota((16, 128), 0)
+    z_here = (lane16 // 32) == lax.rem(row16, 4)
+    row_low = iota((8, 256), 0)
+
     for k in range(5):
         for n in range(len(SHIFTS)):
             faces[k * len(SHIFTS) + n].wait()
             packed[n + 1, k] = face_in[n, k]
 
-
-def earlier(pair, axis):
-    box, ghost = pair
-    if axis == 0:
-        edge = iota((16, 256), 1) % 16 == 0
-        return (
-            jnp.where(edge, pltpu.roll(ghost, 241, 1), pltpu.roll(box, 1, 1)),
-            jnp.where(edge, pltpu.roll(box, 241, 1), pltpu.roll(ghost, 1, 1)),
-        )
-    if axis == 1:
-        box, ghost = pltpu.roll(box, 16, 1), pltpu.roll(ghost, 16, 1)
-        edge = iota((16, 128), 1) < 16
-        low = box[:, :128]
-        return (
-            jnp.concatenate([jnp.where(edge, ghost, low), box[:, 128:]], axis=1),
-            jnp.where(edge, low, ghost),
-        )
-    box, ghost = pltpu.roll(box, 1, 0), pltpu.roll(ghost, 1, 0)
-    edge = iota((8, 256), 0) == 0
-    low = box[:8]
-    return (
-        jnp.concatenate([jnp.where(edge, ghost, low), box[8:]], axis=0),
-        jnp.where(edge, low, ghost),
-    )
-
-
-def later(pair, axis):
-    box, ghost = pair
-    if axis == 0:
-        edge = iota((16, 256), 1) % 16 == 15
-        return (
-            jnp.where(edge, pltpu.roll(ghost, 15, 1), pltpu.roll(box, 255, 1)),
-            jnp.where(edge, pltpu.roll(box, 15, 1), pltpu.roll(ghost, 255, 1)),
-        )
-    if axis == 1:
-        box, ghost = pltpu.roll(box, 240, 1), pltpu.roll(ghost, 112, 1)
-        edge = iota((16, 128), 1) >= 112
-        high = box[:, 128:]
-        return (
-            jnp.concatenate([box[:, :128], jnp.where(edge, ghost, high)], axis=1),
-            jnp.where(edge, high, ghost),
-        )
-    box, ghost = pltpu.roll(box, 15, 0), pltpu.roll(ghost, 7, 0)
-    edge = iota((8, 256), 0) == 7
-    high = box[8:]
-    return (
-        jnp.concatenate([box[:8], jnp.where(edge, ghost, high)], axis=0),
-        jnp.where(edge, high, ghost),
-    )
-
-
-def euler_terms(prim, axis):
-    density, vel, pressure = prim[0], prim[1:4], prim[4]
-    along = vel[axis]
-    energy = pressure * (1.0 / (GAMMA - 1.0)) + 0.5 * density * (
-        vel[0] * vel[0] + vel[1] * vel[1] + vel[2] * vel[2]
-    )
-    conserved = [density, density * vel[0], density * vel[1], density * vel[2], energy]
-    fluxes = [value * along for value in conserved]
-    fluxes[axis + 1] = fluxes[axis + 1] + pressure
-    fluxes[4] = fluxes[4] + pressure * along
-    return conserved, fluxes, jnp.abs(along) + jnp.sqrt(GAMMA * pressure / density)
-
-
-def face_flux(left, right, axis):
-    cons_l, flux_l, speed_l = euler_terms(left, axis)
-    cons_r, flux_r, speed_r = euler_terms(right, axis)
-    speed = jnp.maximum(speed_l, speed_r)
-    return [0.5 * (flux_l[k] + flux_r[k]) - 0.5 * speed * (cons_r[k] - cons_l[k]) for k in range(5)]
-
-
-def sweep(prim, prim_ghost, axis):
-    lefts, rights = ([], []), ([], [])
-    for k in range(5):
-        pair = (prim[k], prim_ghost[k])
-        before = earlier(pair, axis)
-        step = (pair[0] - before[0], pair[1] - before[1])
-        after = later(step, axis)
-        ends = []
-        for i in range(2):
-            slope = jnp.maximum(0.0, jnp.minimum(step[i], after[i])) + jnp.minimum(
-                0.0, jnp.maximum(step[i], after[i])
-            )
-            ends.append(pair[i] + 0.5 * slope)
-            rights[i].append(pair[i] - 0.5 * slope)
-        before = earlier(ends, axis)
-        lefts[0].append(before[0])
-        lefts[1].append(before[1])
-    inner = face_flux(lefts[0], rights[0], axis)
-    outer = face_flux(lefts[1], rights[1], axis)
-    return [later((inner[k], outer[k]), axis)[0] - inner[k] for k in range(5)]
-
-
-def advance_kernel(sizes, moved, packed, top, new_source, ghost, out, where_from):
-    curves, subs = sizes
-    count = curves * subs
-    slots = moved.shape[0]
-    here = lax.axis_index("curve") * subs + lax.axis_index("sub")
-    base = here * slots
-    ranks = [jnp.int32(0)] * 5
-    for j in range(slots):
-        for f in range(6):
-            source = ghost[f, base + j]
-            row, group = jnp.int32(0), jnp.int32(-1)
-            for n, shift in enumerate((0,) + SHIFTS):
-                offset = source - lax.rem(here - shift + count, count) * slots
-                hit = (offset >= 0) & (offset < slots)
-                row = jnp.where(hit, n, row)
-                group = jnp.where(hit, ranks[n], group)
-                ranks[n] = ranks[n] + jnp.where(hit, 1, 0)
-            where_from[0, j * 6 + f] = row
-            where_from[1, j * 6 + f] = group
-    ratio = COURANT / jnp.max(top[...])
-    row_in, column = iota((256, 256), 0), iota((256, 256), 1)
-    x = column % 16
-    low_cell = (column // 16) * 2 + x - 14
-    high_cell = 128 + (column // 16) * 2 + x
-    x_spread = jnp.where(
-        ((x >= 14) & (row_in == low_cell)) | ((x < 2) & (row_in == high_cell)), 1.0, 0.0
-    ).astype(jnp.bfloat16)
-    lane, row16 = iota((16, 128), 1), iota((16, 128), 0)
-    row_wide = iota((8, 256), 0)
-
     @pl.loop(0, slots)
     def _(j):
         def strip(f, k):
-            group = where_from[1, j * 6 + f]
+            group_of = where_from[1, j * 6 + f]
             value = packed[where_from[0, j * 6 + f], k]
-            value = repeated(jnp.where(lane // 32 == group, value, 0.0))
-            return jnp.where(group >= 0, value, FILLER[k])
+            value = repeated(jnp.where(group == group_of, value, 0.0))
+            return jnp.where(group_of >= 0, value, FILLER[k])
 
         def z_lines(f, k):
-            value = jnp.where(lane // 32 == row16 % 4, strip(f, k), 0.0)
+            value = jnp.where(z_here, strip(f, k), 0.0)
             sums = [jnp.sum(value[4 * i : 4 * i + 4], axis=0, keepdims=True) for i in range(4)]
             return [jnp.concatenate(sums[2 * i : 2 * i + 2], axis=1) for i in range(2)]
 
         box = [moved[j, k] for k in range(5)]
         prim = primitives(box)
-        total = None
+        total = [partial[j, k] for k in range(5)]
         for axis in range(3):
             ghosts, sides = [], []
             for k in range(5):
-                if axis < 2:
-                    low, high = strip(2 * axis, k), strip(2 * axis + 1, k)
                 if axis == 0:
-                    sides.append(jnp.concatenate([low, high], axis=1))
+                    sides.append(jnp.concatenate([strip(0, k), strip(1, k)], axis=1))
                 elif axis == 1:
-                    ghosts.append(jnp.where(lane < 64, high, low))
+                    ghosts.append(jnp.where(lane16 < 64, strip(2, k), strip(3, k)))
                 else:
                     low, high = z_lines(4, k), z_lines(5, k)
-                    value = jnp.where(row_wide == 6, low[0], low[1])
-                    value = jnp.where(row_wide == 1, high[1], value)
-                    ghosts.append(jnp.where(row_wide == 0, high[0], value))
+                    value = jnp.where(row_low == 6, high[0], high[1])
+                    value = jnp.where(row_low == 1, low[1], value)
+                    ghosts.append(jnp.where(row_low == 0, low[0], value))
             if axis == 0:
                 spread = picked(jnp.concatenate(sides, axis=0), x_spread)
                 ghosts = [spread[16 * k : 16 * k + 16] for k in range(5)]
-            change = sweep(prim, primitives(ghosts), axis)
-            total = change if total is None else [a + b for a, b in zip(total, change)]
+            rim = []
+            for inside, ghost_value in zip(prim, primitives(ghosts)):
+                if axis == 0:
+                    value = jnp.where(
+                        places[0] < 8, pltpu.roll(inside, 2, 1), pltpu.roll(inside, 254, 1)
+                    )
+                    ends = (places[0] < 2) | (places[0] >= 14)
+                    rim.append(jnp.where(ends, ghost_value, value))
+                elif axis == 1:
+                    low = pltpu.roll(inside, 32, 1)[:, :128]
+                    high = pltpu.roll(inside, 224, 1)[:, 128:]
+                    low = jnp.where(lane16 < 32, ghost_value, low)
+                    high = jnp.where(lane16 >= 96, ghost_value, high)
+                    rim.append(jnp.concatenate([low, high], axis=1))
+                else:
+                    low = jnp.where(row_low < 2, ghost_value, pltpu.roll(inside, 2, 0)[:8])
+                    high = jnp.where(row_low >= 6, ghost_value, pltpu.roll(inside, 14, 0)[8:])
+                    rim.append(jnp.concatenate([low, high], axis=0))
+            change = sweep(rim, axis)
+            up, down, dim = ((2, 254, 1), (32, 224, 1), (2, 14, 0))[axis]
+            for k in range(5):
+                edge = jnp.where(places[axis] >= 14, pltpu.roll(change[k], up, dim), 0.0)
+                edge = jnp.where(places[axis] < 2, pltpu.roll(change[k], down, dim), edge)
+                total[k] = total[k] + edge
         taken = new_source[base + j] >= 0
         for k in range(5):
             out[j, k] = jnp.where(taken, box[k] - ratio * total[k], 0.0)
@@ -400,16 +377,16 @@
     ghost = ghost_source.T
     f32 = jnp.float32
     tile = (5, 16, 128)
-    moved, packed, top = pl.pallas_call(
-        functools.partial(exchange_kernel, sizes),
-        out_shape=[
-            jax.ShapeDtypeStruct(fields.shape, f32),
-            jax.ShapeDtypeStruct((5,) + tile, f32),
-            jax.ShapeDtypeStruct((8, 128), f32),
-        ],
+    return pl.pallas_call(
+        functools.partial(step_kernel, sizes),
+        out_shape=jax.ShapeDtypeStruct(fields.shape, f32),
         in_specs=[pl.BlockSpec(memory_space=pltpu.HBM)] * 3,
-        out_specs=[VMEM] * 3,
+        out_specs=VMEM,
         scratch_shapes=[
+            pltpu.VMEM(fields.shape, f32),
+            pltpu.VMEM((5,) + tile, f32),
+            pltpu.VMEM(fields.shape, f32),
+            pltpu.SMEM((2, slots * 6), jnp.int32),
             pltpu.VMEM(fields.shape, f32),
             pltpu.SMEM(new_source.shape, jnp.int32),
             pltpu.SMEM(ghost.shape, jnp.int32),
@@ -429,17 +406,9 @@
             pltpu.SemaphoreType.DMA((2, curves - 1)),
         ],
         compiler_params=pltpu.CompilerParams(
-            collective_id=0, has_side_effects=True, vmem_limit_bytes=24 << 20
+            collective_id=0, has_side_effects=True, vmem_limit_bytes=60 << 20
         ),
     )(fields, new_source, ghost)
-    return pl.pallas_call(
-        functools.partial(advance_kernel, sizes),
-        out_shape=jax.ShapeDtypeStruct(fields.shape, f32),
-        in_specs=[VMEM, VMEM, VMEM, SMEM, SMEM],
-        out_specs=VMEM,
-        scratch_shapes=[pltpu.SMEM((2, slots * 6), jnp.int32)],
-        compiler_params=pltpu.CompilerParams(vmem_limit_bytes=24 << 20),
-    )(moved, packed, top, new_source, ghost)
 
 
 def solution(mesh):

time: 26.1 us -> 23.8 us (0.912)
  Pallas kernels: 23.6 us -> 22 us
  local copies, waits for them, and re-layouts: 2.28 us -> 1.65 us
    pallas_call x2 -> x1, Pallas kernels: 23.6 us -> 22 us  [body(): pl.pallas_call(functools.partial(step_kernel, sizes), out_shape=jax.Shape...]
    unnamed x6 -> x1, local copies, waits for them, and re-layouts: 2.28 us -> 1.65 us
where the time goes in v3:
time: 23.8 us; the launch traced here: 23.6 us
  Pallas kernels  22 us (92%)
  local copies, waits for them, and re-layouts  1.65 us (7%)
    pallas_call x1, Pallas kernels, body(): pl.pallas_call(functools.partial(step_kernel, sizes), out_shape=jax.Shape...  22 us
    unnamed x1, local copies, waits for them, and re-layouts  1.65 us

profile of v3, /device:TPU:0, one launch (start us, length us, event | category | flops | bytes accessed | tf_op | source)
XLA Modules:
  0.0 23.6 jit_solution(15131006512528613429)
XLA Ops:
  0.0 22.0 %shard_map.37 = f32[3,5,16,256]{3,2,1,0:T(8,128)} custom-call(f32[3,5,16,256]{3,2,1,0:T(8,128)} %fields_hbm.1, s32[96]{0:T(128)} %new_source_hbm.1, s32[6,96]{1,0:T(8,128)} %bitcast.1), custom_call_target="tpu_custom_call" | custom-call | tf_op jit(solution)/shard_map/pallas_call | solution.py:380
  22.0 1.7 %copy.5 = f32[3,5,16,256]{3,2,1,0:T(8,128)} copy(f32[3,5,16,256]{3,2,1,0:T(8,128)} %shard_map.37) | data formatting | bytes 491520

commit v4 on v3

--- a/solution.py
+++ b/solution.py
@@ -14,7 +14,6 @@
 GAMMA = 5.0 / 3.0
 COURANT = 0.3
 FILLER = (1.0, 0.0, 0.0, 0.0, 1.5)
-VMEM = pl.BlockSpec(memory_space=pltpu.VMEM)
 
 
 def iota(shape, dim):
@@ -86,7 +85,7 @@
 
 
 def step_kernel(
-    sizes, fields_hbm, new_source_hbm, ghost_hbm, out, moved, packed, partial, where_from,
+    sizes, fields_hbm, new_source_hbm, ghost_hbm, out_hbm, out, out_sems, moved, packed, partial, where_from,
     fields, new_source, ghost, load_sems, strips, move_out, move_in, face_out, face_in, top_out, top_in, top_out2, top_in2,
     move_sems, face_sems, top_sems, top_sems2,
 ):
@@ -124,6 +123,20 @@
             source = new_source[receiver * slots + j] - base
             pick = jnp.where((source >= 0) & (source < slots), source, pick)
         move_out[n] = fields[pick]
+
+    pl.semaphore_wait(barrier, len(peers))
+
+    moves = []
+    for k in range(5):
+        for n, shift in enumerate((1, -1)):
+            moves.append(
+                pltpu.make_async_remote_copy(
+                    move_out.at[n, k], move_in.at[n, k],
+                    move_sems.at[0, n, k], move_sems.at[1, n, k],
+                    device_id=at(shift), device_id_type=MESH,
+                )
+            )
+            moves[-1].start()
 
     around = [
         new_source[lax.rem(here + s + count, count) * slots + j]
@@ -144,8 +157,6 @@
                 fastest = jnp.maximum(fastest, quick[r : r + 8, c : c + 128])
     top_out[...] = fastest
 
-    pl.semaphore_wait(barrier, len(peers))
-
     firsts = []
     for n, peer in enumerate(sub_peers):
         firsts.append(
@@ -155,18 +166,6 @@
             )
         )
         firsts[-1].start()
-    moves = []
-    for k in range(5):
-        for n, shift in enumerate((1, -1)):
-            moves.append(
-                pltpu.make_async_remote_copy(
-                    move_out.at[n, k], move_in.at[n, k],
-                    move_sems.at[0, n, k], move_sems.at[1, n, k],
-                    device_id=at(shift), device_id_type=MESH,
-                )
-            )
-            moves[-1].start()
-
     loads[2].wait()
     picks = []
     for shift in (0,) + SHIFTS:
@@ -272,14 +271,7 @@
             )
             faces[-1].start()
         packed[0, k] = gathered(picks[0], k)
-        if k == 0:
-            seconds = second_stage()
-    for copy in seconds:
-        copy.wait()
-    fastest = top_out2[...]
-    for n in range(curves - 1):
-        fastest = jnp.maximum(fastest, top_in2[n])
-    ratio = COURANT / jnp.max(fastest)
+    seconds = second_stage()
 
     wide_lane, wide_row = iota((16, 256), 1), iota((16, 256), 0)
     places = (lax.rem(wide_lane, 16), wide_lane // 16, wide_row)
@@ -306,6 +298,12 @@
     z_here = (lane16 // 32) == lax.rem(row16, 4)
     row_low = iota((8, 256), 0)
 
+    for copy in seconds:
+        copy.wait()
+    fastest = top_out2[...]
+    for n in range(curves - 1):
+        fastest = jnp.maximum(fastest, top_in2[n])
+    ratio = COURANT / jnp.max(fastest)
     for k in range(5):
         for n in range(len(SHIFTS)):
             faces[k * len(SHIFTS) + n].wait()
@@ -368,7 +366,11 @@
                 total[k] = total[k] + edge
         taken = new_source[base + j] >= 0
         for k in range(5):
-            out[j, k] = jnp.where(taken, box[k] - ratio * total[k], 0.0)
+            out[j, k] = jnp.where(taken, ratio * total[k] - box[k], 0.0)
+        pltpu.make_async_copy(out.at[j], out_hbm.at[j], out_sems.at[j]).start()
+
+    for j in range(slots):
+        pltpu.make_async_copy(out.at[j], out_hbm.at[j], out_sems.at[j]).wait()
 
 
 def body(sizes, fields, new_source, ghost_source):
@@ -377,12 +379,14 @@
     ghost = ghost_source.T
     f32 = jnp.float32
     tile = (5, 16, 128)
-    return pl.pallas_call(
+    negated = pl.pallas_call(
         functools.partial(step_kernel, sizes),
         out_shape=jax.ShapeDtypeStruct(fields.shape, f32),
         in_specs=[pl.BlockSpec(memory_space=pltpu.HBM)] * 3,
-        out_specs=VMEM,
+        out_specs=pl.BlockSpec(memory_space=pltpu.HBM),
         scratch_shapes=[
+            pltpu.VMEM(fields.shape, f32),
+            pltpu.SemaphoreType.DMA((slots,)),
             pltpu.VMEM(fields.shape, f32),
             pltpu.VMEM((5,) + tile, f32),
             pltpu.VMEM(fields.shape, f32),
@@ -409,6 +413,7 @@
             collective_id=0, has_side_effects=True, vmem_limit_bytes=60 << 20
         ),
     )(fields, new_source, ghost)
+    return -negated
 
 
 def solution(mesh):

time: 23.8 us -> 23.5 us (0.987)
  other arithmetic: 0 us -> 1.66 us
  local copies, waits for them, and re-layouts: 1.65 us -> 0 us
  Pallas kernels: 22 us -> 21.7 us
    neg x0 -> x1, other arithmetic: none -> 1.66 us  [body(): return -negated]
    unnamed x1 -> x0, local copies, waits for them, and re-layouts: 1.65 us -> none
    pallas_call x1, Pallas kernels: 22 us -> 21.7 us  [body(): pl.pallas_call(functools.partial(step_kernel, sizes), out_shape=jax.Shape...]
where the time goes in v4:
time: 23.5 us; the launch traced here: 23.4 us
  Pallas kernels  21.7 us (92%)
  other arithmetic  1.66 us (7%)
    pallas_call x1, Pallas kernels, body(): pl.pallas_call(functools.partial(step_kernel, sizes), out_shape=jax.Shape...  21.7 us
    neg x1, other arithmetic, body(): return -negated  1.66 us

profile of v4, /device:TPU:0, one launch (start us, length us, event | category | flops | bytes accessed | tf_op | source)
XLA Modules:
  0.0 23.4 jit_solution(18036222042062459440)
XLA Ops:
  0.0 21.7 %shard_map.37 = f32[3,5,16,256]{3,2,1,0:T(8,128)} custom-call(f32[3,5,16,256]{3,2,1,0:T(8,128)} %fields_hbm.1, s32[96]{0:T(128)} %new_source_hbm.1, s32[6,96]{1,0:T(8,128)} %bitcast.1), custom_call_target="tpu_custom_call" | custom-call | tf_op jit(solution)/shard_map/pallas_call | solution.py:382
  21.7 1.7 %neg.3 = f32[3,5,16,256]{3,2,1,0:T(8,128)} negate(f32[3,5,16,256]{3,2,1,0:T(8,128)} %shard_map.37) | non-fusion elementwise | flops 61440 | bytes 491520 | tf_op jit(solution)/shard_map/neg | solution.py:416
